TPU v7x, 512 devices: a whole 4x8x8 slice. The times are simulated.
512 devices in a mesh: gx: 8 (over z), gy: 8 (over y_hi, core), gz: 8 (over x, y_lo).
Axes of the slice: x: 4, y: 8 (y_hi: 4, y_lo: 2; y = y_hi * 2 + y_lo), z: 8, core: 2. Of those that a mesh axis runs over, the one named last changes fastest.
Arguments:
- density: float32 [32, 128, 1024], P('gx', 'gy', 'gz'), may hold values from 0.5 to 2
- momentum: float32 [3, 32, 128, 1024], P(None, 'gx', 'gy', 'gz'), may hold values from -1 to 1
- energy: float32 [32, 128, 1024], P('gx', 'gy', 'gz'), may hold values from 3 to 5
- cotangent: bfloat16 [5, 32, 128, 1024], P(None, 'gx', 'gy', 'gz'), may hold values from -6 to 6
- w_in: bfloat16 [64, 30], replicated, may hold values from -1 to 1
- b_in: float32 [64], replicated, may hold values from -3 to 3
- w_out: bfloat16 [5, 64], replicated, may hold values from -0.75 to 0.75
Outputs:
- residual: float32 [5, 32, 128, 1024], P(None, 'gx', 'gy', 'gz')
- state_adjoint: float32 [5, 32, 128, 1024], P(None, 'gx', 'gy', 'gz')
- grad_w_in: float32 [64, 30], replicated
- grad_b_in: float32 [64], replicated
- grad_w_out: float32 [5, 64], replicated
All inputs are finite; a program needn't handle non-finite values.
Results may differ from a plain program's by a relative error of at most 0.025.
Values sent between devices are 32-bit elements; how exact they have to be, the bound alone decides.
A program may use at most 64 MiB of HBM per device.

v0:
```python
import jax
import jax.numpy as jnp
from jax import lax
from jax.sharding import PartitionSpec as P

GAMMA_LESS = 0.4
ALPHA = 4.0
EPSILON = 1e-06


def with_halo(shard, sides, width):
    for axis, dim in sides:
        count, length = (lax.axis_size(axis), shard.shape[dim])
        up = [(i, (i + 1) % count) for i in range(count)]
        down = [(j, i) for i, j in up]
        last = lax.slice_in_dim(shard, length - width, length, axis=dim)
        leading = lax.slice_in_dim(shard, 0, width, axis=dim)
        before = lax.ppermute(last, axis, up)
        after = lax.ppermute(leading, axis, down)
        shard = jnp.concatenate([before, shard, after], axis=dim)
    return shard


def euler_flux(cell, comp):
    density = cell[0]
    momentum = cell[1:4]
    energy = cell[4]
    speed = momentum[comp] / density
    pressure = GAMMA_LESS * (energy - 0.5 * jnp.sum(momentum * momentum, axis=0) / density)
    rows = [momentum[comp]]
    for index in range(3):
        term = momentum[index] * speed
        if index == comp:
            term = term + pressure
        rows.append(term)
    rows.append((energy + pressure) * speed)
    return jnp.stack(rows)


def weno_five(va, vb, vc, ve, vf):
    first = va - 2.0 * vb + vc
    second = vb - 2.0 * vc + ve
    third = vc - 2.0 * ve + vf
    beta_a = 13.0 / 12.0 * first * first + 0.25 * (va - 4.0 * vb + 3.0 * vc) * (
        va - 4.0 * vb + 3.0 * vc
    )
    beta_b = 13.0 / 12.0 * second * second + 0.25 * (vb - ve) * (vb - ve)
    beta_c = 13.0 / 12.0 * third * third + 0.25 * (3.0 * vc - 4.0 * ve + vf) * (
        3.0 * vc - 4.0 * ve + vf
    )
    alpha_a = 0.1 / ((EPSILON + beta_a) * (EPSILON + beta_a))
    alpha_b = 0.6 / ((EPSILON + beta_b) * (EPSILON + beta_b))
    alpha_c = 0.3 / ((EPSILON + beta_c) * (EPSILON + beta_c))
    cand_a = (2.0 * va - 7.0 * vb + 11.0 * vc) / 6.0
    cand_b = (-vb + 5.0 * vc + 2.0 * ve) / 6.0
    cand_c = (2.0 * vc + 5.0 * ve - vf) / 6.0
    return (alpha_a * cand_a + alpha_b * cand_b + alpha_c * cand_c) / (alpha_a + alpha_b + alpha_c)


def product(left, right):
    return jnp.dot(left, right, preferred_element_type=jnp.float32)


def local_pass(padded, lam, dim, w_in, b_in, w_out):
    count = padded.shape[dim] - 6
    faces = count + 1
    comp = dim - 1

    def front(pad):
        cells = [lax.slice_in_dim(pad, k, k + faces, axis=dim) for k in range(6)]
        fluxes = [euler_flux(c, comp) for c in cells]
        plus = [0.5 * (f + ALPHA * c) for f, c in zip(fluxes, cells)]
        minus = [0.5 * (f - ALPHA * c) for f, c in zip(fluxes, cells)]
        weno = weno_five(plus[0], plus[1], plus[2], plus[3], plus[4]) + weno_five(
            minus[5], minus[4], minus[3], minus[2], minus[1]
        )
        return (weno, jnp.concatenate(cells, axis=0))

    (weno, feats), pull = jax.vjp(front, padded)
    feat_shape = feats.shape
    feats_low = feats.astype(jnp.bfloat16).reshape(feat_shape[0], -1)
    pre = product(w_in, feats_low) + b_in[:, None]
    act = jnp.tanh(pre)
    hidden = act.astype(jnp.bfloat16)
    corr = product(w_out, hidden).reshape(weno.shape)
    flux = weno + corr
    div_term = -(
        lax.slice_in_dim(flux, 1, faces, axis=dim) - lax.slice_in_dim(flux, 0, count, axis=dim)
    )
    lam_wide = lam.astype(jnp.float32)
    zero_slab = jnp.zeros_like(lax.slice_in_dim(lam_wide, 0, 1, axis=dim))
    dflux = jnp.concatenate([lam_wide, zero_slab], axis=dim) - jnp.concatenate(
        [zero_slab, lam_wide], axis=dim
    )
    dcorr = dflux.astype(jnp.bfloat16).reshape(5, -1)
    g_w_out = product(dcorr, hidden.T)
    dhid = product(w_out.T, dcorr)
    dpre = (dhid * (1.0 - act * act)).astype(jnp.bfloat16)
    g_w_in = product(dpre, feats_low.T)
    g_b_in = jnp.sum(dpre.astype(jnp.float32), axis=1)
    dfeats = product(w_in.T, dpre).reshape(feat_shape)
    (dpadded,) = pull((dflux, dfeats))
    return (div_term, dpadded, g_w_in, g_b_in, g_w_out)


def sweep(padded, lam, dim, w_in, b_in, w_out):
    other = 2 if dim == 1 else 1
    width = 2
    pieces = padded.shape[other] // width

    def split(arr):
        shape = arr.shape
        arr = arr.reshape(shape[:other] + (pieces, width) + shape[other + 1 :])
        return jnp.moveaxis(arr, other, 0)

    def join(arr):
        arr = jnp.moveaxis(arr, 0, other)
        shape = arr.shape
        return arr.reshape(shape[:other] + (shape[other] * shape[other + 1],) + shape[other + 2 :])

    def single(items):
        return local_pass(items[0], items[1], dim, w_in, b_in, w_out)

    div_term, dpadded, g_w_in, g_b_in, g_w_out = lax.map(single, (split(padded), split(lam)))
    return (
        join(div_term),
        join(dpadded),
        jnp.sum(g_w_in, axis=0),
        jnp.sum(g_b_in, axis=0),
        jnp.sum(g_w_out, axis=0),
    )


def spread_rims(from_left, from_right, count, dim):
    left_widths = [(0, 0)] * 4
    right_widths = [(0, 0)] * 4
    left_widths[dim] = (0, count - 3)
    right_widths[dim] = (count - 3, 0)
    return jnp.pad(from_left, left_widths) + jnp.pad(from_right, right_widths)


def pack_rims(dpadded, dim):
    total = dpadded.shape[dim]
    lower = lax.slice_in_dim(dpadded, 0, 3, axis=dim)
    upper = lax.slice_in_dim(dpadded, total - 3, total, axis=dim)
    return jnp.concatenate([lower, upper], axis=dim)


def settle_rims(dpadded, returned, dim):
    total = dpadded.shape[dim]
    inner = lax.slice_in_dim(dpadded, 3, total - 3, axis=dim)
    from_left = lax.slice_in_dim(returned, 0, 3, axis=dim)
    from_right = lax.slice_in_dim(returned, 9, 12, axis=dim)
    return inner + spread_rims(from_left, from_right, total - 6, dim)


def per_device(density, momentum, energy, cotangent, w_in, b_in, w_out):
    state = jnp.concatenate([density[None], momentum, energy[None]], axis=0)
    padded = with_halo(state, (("gx", 1), ("gy", 2), ("gz", 3)), 3)
    pad_first = padded[:, :, 3:-3, 3:-3]
    pad_second = padded[:, 3:-3, :, 3:-3]
    pad_third = padded[:, 3:-3, 3:-3, :]
    div_first, dpad_first, gwi_first, gbi_first, gwo_first = sweep(
        pad_first, cotangent, 1, w_in, b_in, w_out
    )
    div_second, dpad_second, gwi_second, gbi_second, gwo_second = sweep(
        pad_second, cotangent, 2, w_in, b_in, w_out
    )
    div_third, dpad_third, gwi_third, gbi_third, gwo_third = sweep(
        pad_third, cotangent, 3, w_in, b_in, w_out
    )
    residual = div_first + div_second + div_third
    back_first = with_halo(pack_rims(dpad_first, 1), (("gx", 1),), 3)
    back_second = with_halo(pack_rims(dpad_second, 2), (("gy", 2),), 3)
    back_third = with_halo(pack_rims(dpad_third, 3), (("gz", 3),), 3)
    state_adjoint = (
        settle_rims(dpad_first, back_first, 1)
        + settle_rims(dpad_second, back_second, 2)
        + settle_rims(dpad_third, back_third, 3)
    )
    local_w_in = gwi_first + gwi_second + gwi_third
    local_b_in = gbi_first + gbi_second + gbi_third
    local_w_out = gwo_first + gwo_second + gwo_third
    grad_w_in, grad_b_in, grad_w_out = lax.psum(
        (local_w_in, local_b_in, local_w_out), ("gx", "gy", "gz")
    )
    return (residual, state_adjoint, grad_w_in, grad_b_in, grad_w_out)


def solution(mesh):
    return jax.shard_map(
        per_device,
        mesh=mesh,
        in_specs=(
            P("gx", "gy", "gz"),
            P(None, "gx", "gy", "gz"),
            P("gx", "gy", "gz"),
            P(None, "gx", "gy", "gz"),
            P(),
            P(),
            P(),
        ),
        out_specs=(P(None, "gx", "gy", "gz"), P(None, "gx", "gy", "gz"), P(), P(), P()),
        check_vma=False,
    )
```

profile of v0, /device:TPU:1, one launch (start us, length us, event | category | flops | bytes accessed | tf_op | source)
XLA Modules:
  0.0 385.1 jit_solution(15947219762096711593)
XLA Ops:
  1.6 5.0 %collective-permute-start = (f32[5,3,16,128]{3,2,1,0:T(8,128)S(1)}, f32[5,3,16,128]{3,2,1,0:T(8,128)S(1)}, u32[]{:S(2)}, u32[]{:S(2)}) collective-permute-start(f32[5,3,16,128]{3,2,1,0:T(8,128)S(1)} %get-tuple-element.1419), channel_id=1, source_target_pairs={{0,64},{64,128},{128,192},{192,256},{256,320},{320,384},{384,448},... | collective-permute-start | bytes 368648 | tf_op jit(solution)/shard_map/ppermute | solution.py:18
  6.6 8.6 %collective-permute-start.1 = (f32[5,3,16,128]{3,2,1,0:T(8,128)S(1)}, f32[5,3,16,128]{3,2,1,0:T(8,128)S(1)}, u32[]{:S(2)}, u32[]{:S(2)}) collective-permute-start(f32[5,3,16,128]{3,2,1,0:T(8,128)S(1)} %get-tuple-element.1420), channel_id=1, source_target_pairs={{64,0},{128,64},{192,128},{256,192},{320,256},{384,320},{448,384},... | collective-permute-start | bytes 368648 | tf_op jit(solution)/shard_map/ppermute | solution.py:19
  16.2 2.2 pad_maximum_fusion
  19.2 5.0 %collective-permute-start.2 = (f32[5,10,3,128]{3,2,1,0:T(4,128)}, f32[5,10,3,128]{3,2,1,0:T(4,128)S(1)}, u32[]{:S(2)}, u32[]{:S(2)}) collective-permute-start(f32[5,10,3,128]{3,2,1,0:T(4,128)} %get-tuple-element.1413), channel_id=1, source_target_pairs={{0,8},{8,16},{16,24},{24,32},{32,40},{40,48},{48,56},{56,0},{1,9},... | collective-permute-start | bytes 230408 | tf_op jit(solution)/shard_map/ppermute | solution.py:18
  24.2 1.9 collective-permute-start.3
  26.2 71.5 %while.63 = (s32[]{:T(128)}, f32[8,5,4,2,128]{4,3,2,1,0:T(2,128)S(1)}, f32[8,5,10,2,128]{4,3,2,1,0:T(2,128)S(1)}, f32[8,64,30]{1,2,0:T(8,128)}, f32[8,64]{1,0:T(...) while((s32[]{:T(128)}, ...), condition=%wide.region_8.9_spmd, body=%wide.region_0.8_spmd.sunk | while | flops 22535612 | bytes 10751922 | solution.py:124
  30.3 1.1 convert_reduce_fusion.6
  39.2 1.1 convert_reduce_fusion.6
  48.1 1.1 convert_reduce_fusion.6
  57.1 1.1 convert_reduce_fusion.6
  66.0 1.1 convert_reduce_fusion.6
  75.0 1.1 convert_reduce_fusion.6
  83.9 1.1 convert_reduce_fusion.6
  92.8 1.1 convert_reduce_fusion.6
  99.4 1.9 collective-permute-start.6
  101.3 4.9 %collective-permute-start.7 = (f32[5,3,16,128]{3,2,1,0:T(8,128)}, f32[5,3,16,128]{3,2,1,0:T(8,128)}, u32[]{:S(2)}, u32[]{:S(2)}) collective-permute-start(f32[5,3,16,128]{3,2,1,0:T(8,128)} %get-tuple-element.1412), channel_id=1, source_target_pairs={{64,0},{128,64},{192,128},{256,192},{320,256},{384,320},{448,384},... | collective-permute-start | bytes 368648 | tf_op jit(solution)/shard_map/ppermute | solution.py:19
  107.4 1.5 reduce_sum.354
  109.1 1.2 fusion.362
  112.7 44.1 %while.64 = (s32[]{:T(128)}, f32[2,5,2,16,128]{4,3,2,1,0:T(8,128)}, f32[2,5,2,22,128]{4,3,2,1,0:T(8,128)}, f32[2,64,30]{1,2,0:T(8,128)}, f32[2,64]{1,0:T(2,128)}...) while((s32[]{:T(128)}, f32[2,5,2,16,128]{4,3,2,1,0:T(8,128)}, ...), condition=%wide.region_17.18_spmd, body=%wide.region_9.0_spmd.sunk | while | flops 77589440 | bytes 42266336 | solution.py:124
  116.5 1.0 fusion.525
  119.2 1.2 add_multiply_fusion.90
  121.9 1.2 convert_reduce_fusion.7
  124.1 1.4 fusion.520
  128.4 1.2 multiply_add_fusion.86
  138.6 1.0 fusion.525
  141.2 1.2 add_multiply_fusion.90
  144.0 1.2 convert_reduce_fusion.7
  146.1 1.4 fusion.520
  150.4 1.2 multiply_add_fusion.86
  156.9 1.0 copy.46
  157.9 1.6 copy.38
  159.9 5.5 %collective-permute-start.5 = (f32[5,10,22,3]{2,3,1,0:T(4,128)S(1)}, f32[5,10,22,3]{2,3,1,0:T(4,128)S(1)}, u32[]{:S(2)}, u32[]{:S(2)}) collective-permute-start(f32[5,10,22,3]{2,3,1,0:T(4,128)S(1)} %copy.39), channel_id=1, source_target_pairs={{1,0},{2,1},{3,2},{4,3},{5,4},{6,5},{7,6},{0,7},{9,8},{10,9},{11,1... | collective-permute-start | bytes 39608 | tf_op jit(solution)/shard_map/ppermute | solution.py:19
  165.5 1.9 collective-permute-start.4
  168.7 5.3 %collective-permute-start.8 = (f32[5,4,3,128]{3,2,1,0:T(4,128)}, f32[5,4,3,128]{3,2,1,0:T(4,128)}, u32[]{:S(2)}, u32[]{:S(2)}) collective-permute-start(f32[5,4,3,128]{3,2,1,0:T(4,128)} %get-tuple-element.1417), channel_id=1, source_target_pairs={{0,8},{8,16},{16,24},{24,32},{32,40},{40,48},{48,56},{56,0},{1,9},... | collective-permute-start | bytes 92168 | tf_op jit(solution)/shard_map/ppermute | solution.py:18
  174.5 1.3 reduce_sum.361
  176.4 1.9 collective-permute-start.9
  179.3 1.9 pad_maximum_fusion.3
  183.7 86.3 %while.65 = (s32[]{:T(128)}, f32[2,5,2,16,128]{4,3,2,1,0:T(8,128)}, f32[2,5,2,16,134]{4,3,2,1,0:T(8,128)}, f32[2,64,30]{1,2,0:T(8,128)}, f32[2,64]{1,0:T(2,128)}...) while((s32[]{:T(128)}, f32[2,5,2,16,128]{4,3,2,1,0:T(8,128)}, ...), condition=%wide.region_26.27_spmd, body=%wide.region_18.26_spmd.sunk | while | flops 75946272 | bytes 42301760 | solution.py:124
  192.1 3.3 concatenate.318
  195.5 1.0 fusion.551
  198.3 2.4 add_multiply_fusion.91
  201.4 1.7 reshape.666
  203.1 1.7 fusion.565
  204.8 2.0 convert_reduce_fusion.8
  207.7 1.3 dynamic_update_slice.157
  208.9 1.5 fusion.549
  216.7 2.1 multiply_add_fusion.87
  219.9 1.6 multiply_add_fusion.89
  235.3 3.3 concatenate.318
  238.6 1.0 fusion.551
  241.4 2.4 add_multiply_fusion.91
  244.5 1.7 reshape.666
  246.2 1.7 fusion.565
  248.0 2.0 convert_reduce_fusion.8
  250.8 1.3 dynamic_update_slice.157
  252.1 1.5 fusion.549
  259.9 2.1 multiply_add_fusion.87
  263.1 1.6 multiply_add_fusion.89
  271.0 1.0 copy.47
  272.2 2.3 collective-permute-start.10
  276.0 4.6 %collective-permute-done.10 = f32[5,4,16,3]{3,2,1,0:T(8,128)S(1)} collective-permute-done((f32[5,4,16,3]{3,2,1,0:T(8,128)S(1)}, f32[5,4,16,3]{3,2,1,0:T(8,128)S(1)}, u32[]{:S(2)}, u32[]{:S(2)}) %collective-permute-start.10) | collective-permute-done | bytes 3872 | tf_op jit(solution)/shard_map/ppermute | solution.py:18
  280.6 3.4 collective-permute-start.11
  284.0 99.1 %all-reduce.168 = (f32[64,30]{0,1:T(8,128)}, f32[64]{0:T(128)}, f32[5,64]{1,0:T(8,128)}) all-reduce(f32[64,30]{0,1:T(8,128)S(1)} %add_add_fusion.40, f32[64]{0:T(128)S(1)} %add_add_fusion.42, f32[5,64]{1,0:T(8,128)S(1)} %add_add_fusion.41), channel_id=1, replica_groups=mesh['gx'=8,'gy'=8,'gz'=8] {'gx','gy','gz'}, use_global_device_ids=true, to_apply=%region_30.31 | all-reduce | flops 2304 | bytes 18432 | tf_op jit(solution)/shard_map/psum | solution.py:184
  383.1 1.9 fusion.316
  (1291 shorter events, 155.7 us)
Async XLA Ops:
  1.6 16.8 %copy-start.93 = (f32[3,4,16,128]{3,2,1,0:T(8,128)S(1)}, f32[3,4,16,128]{3,2,1,0:T(8,128)}, u32[]{:S(2)}) copy-start(f32[3,4,16,128]{3,2,1,0:T(8,128)} %param.14) | copy-start | bytes 294916
  1.6 16.8 %copy-start.107 = (f32[4,16,128]{2,1,0:T(8,128)S(1)}, f32[4,16,128]{2,1,0:T(8,128)}, u32[]{:S(2)}) copy-start(f32[4,16,128]{2,1,0:T(8,128)} %param.15) | copy-start | bytes 98308
  1.6 16.8 %copy-start.108 = (f32[4,16,128]{2,1,0:T(8,128)S(1)}, f32[4,16,128]{2,1,0:T(8,128)}, u32[]{:S(2)}) copy-start(f32[4,16,128]{2,1,0:T(8,128)} %param.13) | copy-start | bytes 98308
  1.6 16.7 %collective-permute-start = (f32[5,3,16,128]{3,2,1,0:T(8,128)S(1)}, f32[5,3,16,128]{3,2,1,0:T(8,128)S(1)}, u32[]{:S(2)}, u32[]{:S(2)}) collective-permute-start(f32[5,3,16,128]{3,2,1,0:T(8,128)S(1)} %get-tuple-element.1419), channel_id=1, source_target_pairs={{0,64},{64,128},{128,192},{192,256},{256,320},{320,384},{384,448},... | collective-permute-start | bytes 368648 | tf_op jit(solution)/shard_map/ppermute | solution.py:18
  6.6 11.8 %collective-permute-start.1 = (f32[5,3,16,128]{3,2,1,0:T(8,128)S(1)}, f32[5,3,16,128]{3,2,1,0:T(8,128)S(1)}, u32[]{:S(2)}, u32[]{:S(2)}) collective-permute-start(f32[5,3,16,128]{3,2,1,0:T(8,128)S(1)} %get-tuple-element.1420), channel_id=1, source_target_pairs={{64,0},{128,64},{192,128},{256,192},{320,256},{384,320},{448,384},... | collective-permute-start | bytes 368648 | tf_op jit(solution)/shard_map/ppermute | solution.py:19
  16.2 10.0 %copy-start.27 = (bf16[64,30]{0,1:T(8,128)(2,1)S(1)}, bf16[64,30]{0,1:T(8,128)(2,1)}, u32[]{:S(2)}) copy-start(bf16[64,30]{0,1:T(8,128)(2,1)} %param.17) | copy-start | bytes 11524
  16.2 10.0 %copy-start.123 = (pred[3]{0:T(512)(128)(4,1)S(1)}, pred[3]{0:T(512)(128)(4,1)}, u32[]{:S(2)}) copy-start(pred[3]{0:T(512)(128)(4,1)} %constant.617.clone.1) | copy-start | bytes 13
  18.3 90.6 %copy-start.94 = (f32[5,3,16,128]{3,2,1,0:T(8,128)}, f32[5,3,16,128]{3,2,1,0:T(8,128)S(1)}, u32[]{:S(2)}) copy-start(f32[5,3,16,128]{3,2,1,0:T(8,128)S(1)} %collective-permute-done) | copy-start | bytes 368644
  18.4 90.5 %copy-start.96 = (f32[5,3,16,128]{3,2,1,0:T(8,128)}, f32[5,3,16,128]{3,2,1,0:T(8,128)S(1)}, u32[]{:S(2)}) copy-start(f32[5,3,16,128]{3,2,1,0:T(8,128)S(1)} %collective-permute-done.1) | copy-start | bytes 368644
  19.2 89.7 %collective-permute-start.2 = (f32[5,10,3,128]{3,2,1,0:T(4,128)}, f32[5,10,3,128]{3,2,1,0:T(4,128)S(1)}, u32[]{:S(2)}, u32[]{:S(2)}) collective-permute-start(f32[5,10,3,128]{3,2,1,0:T(4,128)} %get-tuple-element.1413), channel_id=1, source_target_pairs={{0,8},{8,16},{16,24},{24,32},{32,40},{40,48},{48,56},{56,0},{1,9},... | collective-permute-start | bytes 230408 | tf_op jit(solution)/shard_map/ppermute | solution.py:18
  24.2 84.7 %collective-permute-start.3 = (f32[5,10,3,128]{3,2,1,0:T(4,128)}, f32[5,10,3,128]{3,2,1,0:T(4,128)S(1)}, u32[]{:S(2)}, u32[]{:S(2)}) collective-permute-start(f32[5,10,3,128]{3,2,1,0:T(4,128)} %get-tuple-element.1414), channel_id=1, source_target_pairs={{8,0},{16,8},{24,16},{32,24},{40,32},{48,40},{56,48},{0,56},{9,1},... | collective-permute-start | bytes 230408 | tf_op jit(solution)/shard_map/ppermute | solution.py:19
  97.9 11.2 %copy-start.92 = (f32[5,10,8,2,128]{4,3,2,1,0:T(2,128)}, f32[5,10,8,2,128]{4,3,2,1,0:T(2,128)S(1)}, u32[]{:S(2)}) copy-start(f32[5,10,8,2,128]{4,3,2,1,0:T(2,128)S(1)} %copy.45) | copy-start | bytes 1228804
  99.4 283.7 %collective-permute-start.6 = (f32[5,3,16,128]{3,2,1,0:T(8,128)}, f32[5,3,16,128]{3,2,1,0:T(8,128)}, u32[]{:S(2)}, u32[]{:S(2)}) collective-permute-start(f32[5,3,16,128]{3,2,1,0:T(8,128)} %get-tuple-element.1411), channel_id=1, source_target_pairs={{0,64},{64,128},{128,192},{192,256},{256,320},{320,384},{384,448},... | collective-permute-start | bytes 368648 | tf_op jit(solution)/shard_map/ppermute | solution.py:18
  101.3 281.8 %collective-permute-start.7 = (f32[5,3,16,128]{3,2,1,0:T(8,128)}, f32[5,3,16,128]{3,2,1,0:T(8,128)}, u32[]{:S(2)}, u32[]{:S(2)}) collective-permute-start(f32[5,3,16,128]{3,2,1,0:T(8,128)} %get-tuple-element.1412), channel_id=1, source_target_pairs={{64,0},{128,64},{192,128},{256,192},{320,256},{384,320},{448,384},... | collective-permute-start | bytes 368648 | tf_op jit(solution)/shard_map/ppermute | solution.py:19
  114.3 4.9 %copy-start.17 = (f32[5,2,17,128]{3,2,1,0:T(8,128)}, f32[5,2,17,128]{3,2,1,0:T(8,128)S(1)}, u32[]{:S(2)}) copy-start(f32[5,2,17,128]{3,2,1,0:T(8,128)S(1)} %get-tuple-element.2283) | copy-start | bytes 261124 | tf_op jit(solution)/shard_map/while
  114.4 4.7 %copy-start.19 = (f32[5,2,17,128]{3,2,1,0:T(8,128)}, f32[5,2,17,128]{3,2,1,0:T(8,128)S(1)}, u32[]{:S(2)}) copy-start(f32[5,2,17,128]{3,2,1,0:T(8,128)S(1)} %get-tuple-element.2294) | copy-start | bytes 261124 | tf_op jit(solution)/shard_map/while
  136.3 4.9 %copy-start.17 = (f32[5,2,17,128]{3,2,1,0:T(8,128)}, f32[5,2,17,128]{3,2,1,0:T(8,128)S(1)}, u32[]{:S(2)}) copy-start(f32[5,2,17,128]{3,2,1,0:T(8,128)S(1)} %get-tuple-element.2283) | copy-start | bytes 261124 | tf_op jit(solution)/shard_map/while
  136.5 4.7 %copy-start.19 = (f32[5,2,17,128]{3,2,1,0:T(8,128)}, f32[5,2,17,128]{3,2,1,0:T(8,128)S(1)}, u32[]{:S(2)}) copy-start(f32[5,2,17,128]{3,2,1,0:T(8,128)S(1)} %get-tuple-element.2294) | copy-start | bytes 261124 | tf_op jit(solution)/shard_map/while
  156.8 11.2 %copy-start.104 = (f32[2,5,2,16,128]{4,3,2,1,0:T(8,128)S(1)}, f32[2,5,2,16,128]{4,3,2,1,0:T(8,128)}, u32[]{:S(2)}) copy-start(f32[2,5,2,16,128]{4,3,2,1,0:T(8,128)} %get-tuple-element.744) | copy-start | bytes 491524
  156.9 17.1 %copy-start.132 = (f32[2,64]{1,0:T(2,128)S(1)}, f32[2,64]{1,0:T(2,128)}, u32[]{:S(2)}) copy-start(f32[2,64]{1,0:T(2,128)} %get-tuple-element.753) | copy-start | bytes 1540
  156.9 19.0 %copy-start.119 = (f32[2,64,30]{1,2,0:T(8,128)S(1)}, f32[2,64,30]{1,2,0:T(8,128)}, u32[]{:S(2)}) copy-start(f32[2,64,30]{1,2,0:T(8,128)} %get-tuple-element.750) | copy-start | bytes 46084
  157.9 20.9 %copy-start.98 = (f32[5,2,2,22,128]{4,3,2,1,0:T(8,128)}, f32[5,2,2,22,128]{4,3,2,1,0:T(8,128)S(1)}, u32[]{:S(2)}) copy-start(f32[5,2,2,22,128]{4,3,2,1,0:T(8,128)S(1)} %copy.46) | copy-start | bytes 675844
  159.9 19.4 %copy-start.95 = (f32[5,3,16,128]{3,2,1,0:T(8,128)S(1)}, f32[5,3,16,128]{3,2,1,0:T(8,128)}, u32[]{:S(2)}) copy-start(f32[5,3,16,128]{3,2,1,0:T(8,128)} %copy-done.94) | copy-start | bytes 368644
  159.9 19.4 %copy-start.97 = (f32[5,3,16,128]{3,2,1,0:T(8,128)S(1)}, f32[5,3,16,128]{3,2,1,0:T(8,128)}, u32[]{:S(2)}) copy-start(f32[5,3,16,128]{3,2,1,0:T(8,128)} %copy-done.96) | copy-start | bytes 368644
  159.9 19.4 %copy-start.110 = (f32[5,10,3,128]{3,2,1,0:T(4,128)S(1)}, f32[5,10,3,128]{3,2,1,0:T(4,128)}, u32[]{:S(2)}) copy-start(f32[5,10,3,128]{3,2,1,0:T(4,128)} %copy-done.109) | copy-start | bytes 230404
  159.9 19.4 %copy-start.112 = (f32[5,10,3,128]{3,2,1,0:T(4,128)S(1)}, f32[5,10,3,128]{3,2,1,0:T(4,128)}, u32[]{:S(2)}) copy-start(f32[5,10,3,128]{3,2,1,0:T(4,128)} %copy-done.111) | copy-start | bytes 230404
  159.9 18.9 %collective-permute-start.5 = (f32[5,10,22,3]{2,3,1,0:T(4,128)S(1)}, f32[5,10,22,3]{2,3,1,0:T(4,128)S(1)}, u32[]{:S(2)}, u32[]{:S(2)}) collective-permute-start(f32[5,10,22,3]{2,3,1,0:T(4,128)S(1)} %copy.39), channel_id=1, source_target_pairs={{1,0},{2,1},{3,2},{4,3},{5,4},{6,5},{7,6},{0,7},{9,8},{10,9},{11,1... | collective-permute-start | bytes 39608 | tf_op jit(solution)/shard_map/ppermute | solution.py:19
  165.5 11.0 %collective-permute-start.4 = (f32[5,10,22,3]{2,3,1,0:T(4,128)S(1)}, f32[5,10,22,3]{2,3,1,0:T(4,128)S(1)}, u32[]{:S(2)}, u32[]{:S(2)}) collective-permute-start(f32[5,10,22,3]{2,3,1,0:T(4,128)S(1)} %copy.38), channel_id=1, source_target_pairs={{0,1},{1,2},{2,3},{3,4},{4,5},{5,6},{6,7},{7,0},{8,9},{9,10},{10,1... | collective-permute-start | bytes 39608 | tf_op jit(solution)/shard_map/ppermute | solution.py:18
  168.7 214.4 %collective-permute-start.8 = (f32[5,4,3,128]{3,2,1,0:T(4,128)}, f32[5,4,3,128]{3,2,1,0:T(4,128)}, u32[]{:S(2)}, u32[]{:S(2)}) collective-permute-start(f32[5,4,3,128]{3,2,1,0:T(4,128)} %get-tuple-element.1417), channel_id=1, source_target_pairs={{0,8},{8,16},{16,24},{24,32},{32,40},{40,48},{48,56},{56,0},{1,9},... | collective-permute-start | bytes 92168 | tf_op jit(solution)/shard_map/ppermute | solution.py:18
  176.4 206.7 %collective-permute-start.9 = (f32[5,4,3,128]{3,2,1,0:T(4,128)}, f32[5,4,3,128]{3,2,1,0:T(4,128)}, u32[]{:S(2)}, u32[]{:S(2)}) collective-permute-start(f32[5,4,3,128]{3,2,1,0:T(4,128)} %get-tuple-element.1418), channel_id=1, source_target_pairs={{8,0},{16,8},{24,16},{32,24},{40,32},{48,40},{56,48},{0,56},{9,1},... | collective-permute-start | bytes 92168 | tf_op jit(solution)/shard_map/ppermute | solution.py:19
  186.0 3.9 %copy-start.36 = (f32[2,16,129]{2,1,0:T(8,128)}, f32[2,16,129]{2,1,0:T(8,128)S(1)}, u32[]{:S(2)}) copy-start(f32[2,16,129]{2,1,0:T(8,128)S(1)} %get-tuple-element.2454) | copy-start | bytes 49540 | tf_op jit(solution)/shard_map/while
  186.0 4.0 %copy-start.40 = (f32[2,16,129]{2,1,0:T(8,128)}, f32[2,16,129]{2,1,0:T(8,128)S(1)}, u32[]{:S(2)}) copy-start(f32[2,16,129]{2,1,0:T(8,128)S(1)} %get-tuple-element.2460) | copy-start | bytes 49540 | tf_op jit(solution)/shard_map/while
  189.7 8.6 %copy-start.3 = (f32[5,2,16,129]{3,2,1,0:T(8,128)}, f32[5,2,16,129]{3,2,1,0:T(8,128)S(1)}, u32[]{:S(2)}) copy-start(f32[5,2,16,129]{3,2,1,0:T(8,128)S(1)} %get-tuple-element.2448) | copy-start | bytes 247684 | tf_op jit(solution)/shard_map/while
  189.7 8.6 %copy-start.7 = (f32[5,2,16,129]{3,2,1,0:T(8,128)}, f32[5,2,16,129]{3,2,1,0:T(8,128)S(1)}, u32[]{:S(2)}) copy-start(f32[5,2,16,129]{3,2,1,0:T(8,128)S(1)} %get-tuple-element.2466) | copy-start | bytes 247684 | tf_op jit(solution)/shard_map/while
  189.9 7.5 %copy-start.2 = (f32[1,2,16,129]{3,2,1,0:T(8,128)}, f32[1,2,16,129]{3,2,1,0:T(8,128)S(1)}, u32[]{:S(2)}) copy-start(f32[1,2,16,129]{3,2,1,0:T(8,128)S(1)} %get-tuple-element.2456) | copy-start | bytes 49540 | tf_op jit(solution)/shard_map/while
  190.3 8.0 %copy-start.5 = (f32[5,2,16,129]{3,2,1,0:T(8,128)}, f32[5,2,16,129]{3,2,1,0:T(8,128)S(1)}, u32[]{:S(2)}) copy-start(f32[5,2,16,129]{3,2,1,0:T(8,128)S(1)} %get-tuple-element.2464) | copy-start | bytes 247684 | tf_op jit(solution)/shard_map/while
  206.8 3.7 copy-start.38
  211.3 5.4 %copy-start.4 = (f32[5,2,16,129]{3,2,1,0:T(8,128)S(1)}, f32[5,2,16,129]{3,2,1,0:T(8,128)}, u32[]{:S(2)}) copy-start(f32[5,2,16,129]{3,2,1,0:T(8,128)} %copy-done.3) | copy-start | bytes 247684 | tf_op jit(solution)/shard_map/while
  211.3 5.4 %copy-start.6 = (f32[5,2,16,129]{3,2,1,0:T(8,128)S(1)}, f32[5,2,16,129]{3,2,1,0:T(8,128)}, u32[]{:S(2)}) copy-start(f32[5,2,16,129]{3,2,1,0:T(8,128)} %copy-done.5) | copy-start | bytes 247684 | tf_op jit(solution)/shard_map/while
  211.3 5.3 %copy-start.8 = (f32[5,2,16,129]{3,2,1,0:T(8,128)S(1)}, f32[5,2,16,129]{3,2,1,0:T(8,128)}, u32[]{:S(2)}) copy-start(f32[5,2,16,129]{3,2,1,0:T(8,128)} %copy-done.7) | copy-start | bytes 247684 | tf_op jit(solution)/shard_map/while
  211.3 5.3 %copy-start.51 = (f32[5,2,16,129]{3,2,1,0:T(8,128)S(1)}, f32[5,2,16,129]{3,2,1,0:T(8,128)}, u32[]{:S(2)}) copy-start(f32[5,2,16,129]{3,2,1,0:T(8,128)} %copy-done.50) | copy-start | bytes 247684 | tf_op jit(solution)/shard_map/while
  229.1 3.9 %copy-start.36 = (f32[2,16,129]{2,1,0:T(8,128)}, f32[2,16,129]{2,1,0:T(8,128)S(1)}, u32[]{:S(2)}) copy-start(f32[2,16,129]{2,1,0:T(8,128)S(1)} %get-tuple-element.2454) | copy-start | bytes 49540 | tf_op jit(solution)/shard_map/while
  229.1 4.0 %copy-start.40 = (f32[2,16,129]{2,1,0:T(8,128)}, f32[2,16,129]{2,1,0:T(8,128)S(1)}, u32[]{:S(2)}) copy-start(f32[2,16,129]{2,1,0:T(8,128)S(1)} %get-tuple-element.2460) | copy-start | bytes 49540 | tf_op jit(solution)/shard_map/while
  232.8 8.6 %copy-start.3 = (f32[5,2,16,129]{3,2,1,0:T(8,128)}, f32[5,2,16,129]{3,2,1,0:T(8,128)S(1)}, u32[]{:S(2)}) copy-start(f32[5,2,16,129]{3,2,1,0:T(8,128)S(1)} %get-tuple-element.2448) | copy-start | bytes 247684 | tf_op jit(solution)/shard_map/while
  232.8 8.6 %copy-start.7 = (f32[5,2,16,129]{3,2,1,0:T(8,128)}, f32[5,2,16,129]{3,2,1,0:T(8,128)S(1)}, u32[]{:S(2)}) copy-start(f32[5,2,16,129]{3,2,1,0:T(8,128)S(1)} %get-tuple-element.2466) | copy-start | bytes 247684 | tf_op jit(solution)/shard_map/while
  233.0 7.5 %copy-start.2 = (f32[1,2,16,129]{3,2,1,0:T(8,128)}, f32[1,2,16,129]{3,2,1,0:T(8,128)S(1)}, u32[]{:S(2)}) copy-start(f32[1,2,16,129]{3,2,1,0:T(8,128)S(1)} %get-tuple-element.2456) | copy-start | bytes 49540 | tf_op jit(solution)/shard_map/while
  233.4 8.0 %copy-start.5 = (f32[5,2,16,129]{3,2,1,0:T(8,128)}, f32[5,2,16,129]{3,2,1,0:T(8,128)S(1)}, u32[]{:S(2)}) copy-start(f32[5,2,16,129]{3,2,1,0:T(8,128)S(1)} %get-tuple-element.2464) | copy-start | bytes 247684 | tf_op jit(solution)/shard_map/while
  254.4 5.4 %copy-start.4 = (f32[5,2,16,129]{3,2,1,0:T(8,128)S(1)}, f32[5,2,16,129]{3,2,1,0:T(8,128)}, u32[]{:S(2)}) copy-start(f32[5,2,16,129]{3,2,1,0:T(8,128)} %copy-done.3) | copy-start | bytes 247684 | tf_op jit(solution)/shard_map/while
  254.5 5.4 %copy-start.6 = (f32[5,2,16,129]{3,2,1,0:T(8,128)S(1)}, f32[5,2,16,129]{3,2,1,0:T(8,128)}, u32[]{:S(2)}) copy-start(f32[5,2,16,129]{3,2,1,0:T(8,128)} %copy-done.5) | copy-start | bytes 247684 | tf_op jit(solution)/shard_map/while
  254.5 5.3 %copy-start.8 = (f32[5,2,16,129]{3,2,1,0:T(8,128)S(1)}, f32[5,2,16,129]{3,2,1,0:T(8,128)}, u32[]{:S(2)}) copy-start(f32[5,2,16,129]{3,2,1,0:T(8,128)} %copy-done.7) | copy-start | bytes 247684 | tf_op jit(solution)/shard_map/while
  254.5 5.3 %copy-start.51 = (f32[5,2,16,129]{3,2,1,0:T(8,128)S(1)}, f32[5,2,16,129]{3,2,1,0:T(8,128)}, u32[]{:S(2)}) copy-start(f32[5,2,16,129]{3,2,1,0:T(8,128)} %copy-done.50) | copy-start | bytes 247684 | tf_op jit(solution)/shard_map/while
  270.0 5.2 %copy-start.122 = (f32[2,64,30]{1,2,0:T(8,128)S(1)}, f32[2,64,30]{1,2,0:T(8,128)}, u32[]{:S(2)}) copy-start(f32[2,64,30]{1,2,0:T(8,128)} %get-tuple-element.751) | copy-start | bytes 46084
  270.0 5.3 %copy-start.100 = (f32[5,4,8,2,128]{4,3,2,1,0:T(2,128)S(1)}, f32[5,4,8,2,128]{4,3,2,1,0:T(2,128)}, u32[]{:S(2)}) copy-start(f32[5,4,8,2,128]{4,3,2,1,0:T(2,128)} %copy.33) | copy-start | bytes 491524
  270.0 5.3 %copy-start.101 = (f32[5,2,2,16,128]{4,3,2,1,0:T(8,128)S(1)}, f32[5,2,2,16,128]{4,3,2,1,0:T(8,128)}, u32[]{:S(2)}) copy-start(f32[5,2,2,16,128]{4,3,2,1,0:T(8,128)} %copy.37) | copy-start | bytes 491524
  270.0 6.0 %copy-start.124 = (f32[64,30]{0,1:T(8,128)S(1)}, f32[64,30]{0,1:T(8,128)}, u32[]{:S(2)}) copy-start(f32[64,30]{0,1:T(8,128)} %reduce_sum.354) | copy-start | bytes 23044
  270.0 6.0 %copy-start.125 = (f32[64,30]{0,1:T(8,128)S(1)}, f32[64,30]{0,1:T(8,128)}, u32[]{:S(2)}) copy-start(f32[64,30]{0,1:T(8,128)} %reduce_sum.355) | copy-start | bytes 23044
  271.0 5.0 %copy-start.126 = (f32[5,64]{1,0:T(8,128)S(1)}, f32[5,64]{1,0:T(8,128)}, u32[]{:S(2)}) copy-start(f32[5,64]{1,0:T(8,128)} %reduce_sum.360) | copy-start | bytes 3844
  271.0 5.0 %copy-start.127 = (f32[5,64]{1,0:T(8,128)S(1)}, f32[5,64]{1,0:T(8,128)}, u32[]{:S(2)}) copy-start(f32[5,64]{1,0:T(8,128)} %reduce_sum.361) | copy-start | bytes 3844
  271.0 5.0 %copy-start.133 = (f32[2,64]{1,0:T(2,128)S(1)}, f32[2,64]{1,0:T(2,128)}, u32[]{:S(2)}) copy-start(f32[2,64]{1,0:T(2,128)} %get-tuple-element.754) | copy-start | bytes 1540
  271.0 13.0 %copy-start.128 = (f32[64]{0:T(128)S(1)}, f32[64]{0:T(128)}, u32[]{:S(2)}) copy-start(f32[64]{0:T(128)} %reduce_sum.357) | copy-start | bytes 772
  271.0 13.0 %copy-start.129 = (f32[64]{0:T(128)S(1)}, f32[64]{0:T(128)}, u32[]{:S(2)}) copy-start(f32[64]{0:T(128)} %reduce_sum.358) | copy-start | bytes 772
  271.0 112.1 %copy-start.99 = (f32[5,2,2,22,128]{4,3,2,1,0:T(8,128)S(1)}, f32[5,2,2,22,128]{4,3,2,1,0:T(8,128)}, u32[]{:S(2)}) copy-start(f32[5,2,2,22,128]{4,3,2,1,0:T(8,128)} %copy-done.98) | copy-start | bytes 675844
  272.2 8.4 %collective-permute-start.10 = (f32[5,4,16,3]{3,2,1,0:T(8,128)S(1)}, f32[5,4,16,3]{3,2,1,0:T(8,128)S(1)}, u32[]{:S(2)}, u32[]{:S(2)}) collective-permute-start(f32[5,4,16,3]{3,2,1,0:T(8,128)S(1)} %get-tuple-element.1415), channel_id=1, source_target_pairs={{0,1},{1,2},{2,3},{3,4},{4,5},{5,6},{6,7},{7,0},{8,9},{9,10},{10,1... | collective-permute-start | bytes 11528 | tf_op jit(solution)/shard_map/ppermute | solution.py:18
  280.6 102.5 %collective-permute-start.11 = (f32[5,4,16,3]{3,2,1,0:T(8,128)S(1)}, f32[5,4,16,3]{3,2,1,0:T(8,128)S(1)}, u32[]{:S(2)}, u32[]{:S(2)}) collective-permute-start(f32[5,4,16,3]{3,2,1,0:T(8,128)S(1)} %get-tuple-element.1416), channel_id=1, source_target_pairs={{1,0},{2,1},{3,2},{4,3},{5,4},{6,5},{7,6},{0,7},{9,8},{10,9},{11,1... | collective-permute-start | bytes 11528 | tf_op jit(solution)/shard_map/ppermute | solution.py:19
  (186 other events, 220.2 us)
where the time goes:
time: 389 us; the launch traced here: 385 us
  blocking collectives  99.1 us (25%)
  other arithmetic  88.7 us (23%)
  local copies, waits for them, and re-layouts  86.4 us (22%)
  matrix products  52 us (13%)
  starting transfers between devices  47.6 us (12%)
  loops' own time  5.39 us (1%)
  waiting for transfers between devices  4.61 us (1%)
    psum x1, blocking collectives, per_device(): lax.psum((local_w_in, local_b_in, local_w_out), ('gx', 'gy', 'gz'))  99.1 us
    dot_general x72, matrix products, product(): return jnp.dot(left, right, preferred_element_type=jnp.float32)  52 us
    ppermute x6, starting transfers between devices, with_halo(): after = lax.ppermute(leading, axis, down)  26.2 us
    add_any x42, other arithmetic, front(): plus = [0.5 * (f + ALPHA * c) for f, c in zip(fluxes, cells)]  25.8 us
    while x428, local copies, waits for them, and re-layouts  25.3 us
    ppermute x6, starting transfers between devices, with_halo(): before = lax.ppermute(last, axis, up)  21.4 us
    concatenate x84, local copies, waits for them, and re-layouts, front(): return (weno, jnp.concatenate(cells, axis=0))  16.3 us
    split x84, local copies, waits for them, and re-layouts, front(): return (weno, jnp.concatenate(cells, axis=0))  15.1 us
  transfers between devices with their start and end apart: 12, of which 1 were waited for; matrix products, arithmetic and copies ran while one was open for 52% of the time, Pallas kernels for 0%

commit v1 on v0

v1 whole, which is shorter than its diff:
```python
import functools

import jax
import jax.numpy as jnp
from jax import lax
from jax.experimental import pallas as pl
from jax.experimental.pallas import tpu as pltpu
from jax.sharding import PartitionSpec as P

F32 = jnp.float32
BF16 = jnp.bfloat16
AXES = ("gx", "gy", "gz")
MESH = pl.DeviceIdType.MESH
EPSILON = 1e-06
XC = 14
NT = (((1,), (1,)), ((), ()))


def recip(value):
    guess = pl.reciprocal(value, approx=True)
    return guess * (2.0 - value * guess)


def dot(left, right):
    return jnp.dot(left, right, preferred_element_type=F32)


def dot_nt(left, right):
    return lax.dot_general(left, right, NT, preferred_element_type=F32)


def line_weno(cells, cots):
    faces = len(cots)
    total = len(cells)
    diff = [cells[i + 1] - cells[i] for i in range(total - 1)]
    second = [None] + [diff[i] - diff[i - 1] for i in range(1, total - 1)]
    half = [None] + [0.5 * s for s in second[1:]]
    square = [None] + [EPSILON + (13.0 / 12.0) * s * s for s in second[1:]]
    third = [None] + [second[i + 1] - second[i] for i in range(1, total - 2)]
    values = []
    d_cell = [None] * total
    d_diff = [None] * total
    d_half = [None] * total
    d_square = [None] * total
    d_third = [None] * total

    def add(store, index, value):
        store[index] = value if store[index] is None else store[index] + value

    for k in range(faces):
        d1, d2 = diff[k + 1], diff[k + 2]
        t1, t2 = third[k + 1], third[k + 2]
        twice = t1 + t1
        pa = d1 + half[k + 1]
        pb = 0.5 * (d1 + d2)
        pc = d2 - half[k + 3]
        ra = recip(square[k + 1] + pa * pa)
        rb = recip(square[k + 2] + pb * pb)
        rc = recip(square[k + 3] + pc * pc)
        wa = ra * ra
        wb = 6.0 * (rb * rb)
        wc = 3.0 * (rc * rc)
        norm = recip(wa + wb + wc)
        y = (wa * twice + wc * t2) * norm
        values.append(cells[k + 2] + (1.0 / 6.0) * (d1 + (d2 + d2) - y))
        g = cots[k]
        sixth = (1.0 / 6.0) * g
        gn = sixth * norm
        ga = gn * wa
        gb = gn * wb
        gc = gn * wc
        ta = ga * ra * (twice - y)
        tb = gb * rb * y
        tc = gc * rc * (t2 - y)
        qa = 4.0 * (pa * ta)
        qb = 2.0 * (pb * tb)
        qc = 4.0 * (pc * tc)
        add(d_cell, k + 2, g)
        add(d_diff, k + 1, sixth + qa - qb)
        add(d_diff, k + 2, (sixth + sixth) + qc - qb)
        add(d_half, k + 1, qa)
        add(d_half, k + 3, -qc)
        add(d_square, k + 1, ta)
        add(d_square, k + 2, -tb)
        add(d_square, k + 3, tc)
        add(d_third, k + 1, -(ga + ga))
        add(d_third, k + 2, -gc)
    for i in range(1, total - 1):
        value = (13.0 / 3.0) * second[i] * d_square[i]
        if d_half[i] is not None:
            value = value + 0.5 * d_half[i]
        if d_third[i - 1] is not None:
            value = value + d_third[i - 1]
        if d_third[i] is not None:
            value = value - d_third[i]
        add(d_diff, i, value)
        add(d_diff, i - 1, -value)
    for i in range(total - 1):
        add(d_cell, i + 1, d_diff[i])
        add(d_cell, i, -d_diff[i])
    return values, d_cell


def kernel(
    sizes, dens, mom, ener, cot, w_in, b_in, w_out,
    res_o, adj_o, gwi_o, gbi_o, gwo_o,
    nat, lamn, vv, ll, fp, fm, dfp, dfm, dv, corr_s, res_s,
    zw, zl, w1, w1t, w2, w2t, hid, dpr, g1, g2, gm, ar, ar_in,
    ys, yr, zs, zr, xr, yb, ybr, zb, zbr, xbr,
    halo_send, halo_recv, back_send, back_recv, ar_send, ar_recv,
):
    me = [lax.axis_index(a) for a in AXES]

    def peer(axis, step):
        count = sizes[axis]
        return {AXES[axis]: lax.rem(me[axis] + (step % count), count)}

    bar = pltpu.get_barrier_semaphore()
    for axis in range(3):
        for step in range(1, sizes[axis]):
            pl.semaphore_signal(bar, 1, device_id=peer(axis, step), device_id_type=MESH)

    lane = lax.broadcasted_iota(jnp.int32, (64, 128), 1)
    low = lane < 64
    lane8 = lax.broadcasted_iota(jnp.int32, (3, 128), 1)
    low3 = lane8 < 64

    nat[0] = dens[...]
    nat[1:4] = mom[...]
    nat[4] = ener[...]
    lamn[...] = cot[...].astype(F32)

    def swap(value):
        return pltpu.roll(value, 64, 1)

    fields = [(nat, zw, 3, v) for v in range(5)] + [(lamn, zl, 0, v) for v in range(5)]
    for first, second in zip(fields[0::2], fields[1::2]):
        both = jnp.concatenate([first[0][first[3]], second[0][second[3]]], axis=0)
        turned = jnp.transpose(both)
        upper, lower = turned[0:64], turned[64:128]
        first[1][first[3], first[2] : first[2] + 64, :] = jnp.where(low, upper, swap(lower))
        second[1][second[3], second[2] : second[2] + 64, :] = jnp.where(low, swap(upper), lower)
    for v in range(5):
        zs[0, 3 * v : 3 * v + 3, :] = zw[v, 3:6, :]
        zs[1, 3 * v : 3 * v + 3, :] = zw[v, 64:67, :]
        for j in range(3):
            at = (3 * v + j) * 4
            ys[0, at : at + 4, :] = nat[v, pl.ds(j, 4, stride=16), :]
            ys[1, at : at + 4, :] = nat[v, pl.ds(13 + j, 4, stride=16), :]

    pl.semaphore_wait(bar, sum(sizes) - 3)

    def remote(src, dst, send, recv, index, axis, step):
        return pltpu.make_async_remote_copy(
            src_ref=src, dst_ref=dst, send_sem=send.at[index], recv_sem=recv.at[index],
            device_id=peer(axis, step), device_id_type=MESH,
        )

    halo = [
        remote(nat.at[:, 0:48, :], xr.at[1], halo_send, halo_recv, 0, 0, -1),
        remote(nat.at[:, 16:64, :], xr.at[0], halo_send, halo_recv, 1, 0, 1),
        remote(ys.at[0], yr.at[1], halo_send, halo_recv, 2, 1, -1),
        remote(ys.at[1], yr.at[0], halo_send, halo_recv, 3, 1, 1),
        remote(zs.at[0], zr.at[1], halo_send, halo_recv, 4, 2, -1),
        remote(zs.at[1], zr.at[0], halo_send, halo_recv, 5, 2, 1),
    ]
    for copy in halo:
        copy.start()

    def iota(shape, dim):
        return lax.broadcasted_iota(jnp.int32, shape, dim)

    def one_hot(shape, wide):
        return (iota(shape, wide) // 8 == iota(shape, 1 - wide)).astype(F32).astype(BF16)

    def same_row(shape):
        return (iota(shape, 0) % 8) == (iota(shape, 1) % 8)

    spread = one_hot((512, 64), 0)
    spread_t = one_hot((64, 512), 1)
    bias = b_in[...]
    bias_a = bias.astype(BF16).astype(F32)
    bias_b = (bias - bias_a).astype(BF16).astype(F32)
    bias_c = bias - bias_a - bias_b
    row = iota((256, 64), 0)
    bias_rows = jnp.where(row == 240, bias_a, jnp.where(row == 241, bias_b, jnp.where(row == 242, bias_c, 0.0)))
    wide_in = dot(w_in[...], one_hot((30, 256), 1)).astype(BF16)
    full_in = jnp.where(same_row((512, 256)), dot(spread, wide_in), 0.0)
    w1[...] = (full_in + dot_nt(spread, bias_rows.astype(BF16))).astype(BF16)
    tall_in = dot_nt(one_hot((240, 30), 0), w_in[...]).astype(BF16)
    w1t[...] = jnp.where(same_row((240, 512)), dot(tall_in, spread_t), 0.0).astype(BF16)
    tall_out = dot(one_hot((48, 5), 0), w_out[...]).astype(BF16)
    w2[...] = jnp.where(same_row((48, 512)), dot(tall_out, spread_t), 0.0).astype(BF16)
    wide_out = dot_nt(spread, w_out[...]).astype(BF16)
    w2t[...] = jnp.where(same_row((512, 48)), dot(wide_out, one_hot((5, 48), 1)), 0.0).astype(BF16)

    for v in range(5):
        for i in range(4):
            for t in range(2):
                at = i * 16 + t * 8
                vv[XC + 3 + i, 5 * t + v] = nat[v, at : at + 8, :]
                ll[11 + i, 5 * t + v] = lamn[v, at : at + 8, :]
        for r in range(14):
            for h in range(2):
                y = 8 * h + r - 3
                if 0 <= y < 16:
                    vv[r, v, 4 * h : 4 * h + 4, :] = nat[v, pl.ds(y, 4, stride=16), :]
        for j in range(8):
            vv[3 + j, 5 + v] = zw[v, pl.ds(3 + j, 8, stride=8), :]
            ll[1 + j, 5 + v] = zl[v, pl.ds(j, 8, stride=8), :]
            for h in range(2):
                ll[1 + j, v, 4 * h : 4 * h + 4, :] = lamn[v, pl.ds(8 * h + j, 4, stride=16), :]
    for end in (0, 9, 10, 15):
        ll[end] = jnp.zeros((10, 8, 128), F32)
    dv[...] = jnp.zeros(dv.shape, F32)
    g1[...] = jnp.zeros(g1.shape, F32)
    g2[...] = jnp.zeros(g2.shape, F32)

    for copy in halo[2:]:
        copy.wait_recv()
    for v in range(5):
        for j in range(3):
            at = (3 * v + j) * 4
            vv[j, v, 0:4, :] = yr[0, at : at + 4, :]
            vv[11 + j, v, 4:8, :] = yr[1, at : at + 4, :]
        zw[v, 0:3, :] = swap(jnp.where(low3, zw[v, 64:67, :], zr[0, 3 * v : 3 * v + 3, :]))
        zw[v, 67:70, :] = swap(jnp.where(low3, zr[1, 3 * v : 3 * v + 3, :], zw[v, 3:6, :]))
        for r in (0, 1, 2, 11, 12, 13):
            vv[r, 5 + v] = zw[v, pl.ds(r, 8, stride=8), :]

    ones = jnp.ones((16, 256), BF16)
    blank = jnp.zeros((8, 256), F32)

    def network(p, c0, lb):
        cells = [vv[pl.ds(c0, 6), 5 * t : 5 * t + 5].reshape(240, 128) for t in range(2)]
        feats = jnp.concatenate([jnp.concatenate(cells, axis=1).astype(BF16), ones], axis=0)
        steps = [(ll[lb + 1, 5 * t : 5 * t + 5] - ll[lb, 5 * t : 5 * t + 5]).reshape(40, 128) for t in range(2)]
        dcorr = jnp.concatenate([jnp.concatenate(steps, axis=1), blank], axis=0).astype(BF16)
        for part in range(4):
            rows = pl.ds(128 * part, 128)
            act = jnp.tanh(dot(w1[rows, :], feats))
            hid[rows, :] = act.astype(BF16)
            dpr[rows, :] = (dot(w2t[rows, :], dcorr) * (1.0 - act * act)).astype(BF16)
        corr = dot(w2[...], hid[...])
        dfeat = dot(w1t[...], dpr[...])
        for t in range(2):
            lanes = slice(128 * t, 128 * t + 128)
            corr_s[p, 5 * t : 5 * t + 5] = corr[0:40, lanes].reshape(5, 8, 128)
            dv[pl.ds(c0, 6), 5 * t : 5 * t + 5] += dfeat[:, lanes].reshape(6, 5, 8, 128)
        g1[...] += dot_nt(feats, dpr[...])
        g2[...] += dot_nt(dcorr, hid[...])

    def net_yz(p, carry):
        network(p, p, p)
        return carry

    lax.fori_loop(0, 9, net_yz, 0)

    for copy in halo[:2]:
        copy.wait_recv()
    for v in range(5):
        for i in range(3):
            for t in range(2):
                at = i * 16 + t * 8
                vv[XC + i, 5 * t + v] = xr[0, v, at : at + 8, :]
                vv[XC + 7 + i, 5 * t + v] = xr[1, v, at : at + 8, :]

    def net_x(k, carry):
        network(9 + k, XC + k, 10 + k)
        return carry

    lax.fori_loop(0, 5, net_x, 0)

    inner = jnp.where(same_row((240, 512)), g1[0:240, :], 0.0).reshape(30, 8, 512)
    outer = jnp.where(same_row((40, 512)), g2[0:40, :], 0.0).reshape(5, 8, 512)
    gm[0:30, :] = jnp.sum(inner, axis=1)
    gm[30:31, :] = g1[240:241, :]
    gm[31:36, :] = jnp.sum(outer, axis=1)
    gm[36:40, :] = jnp.zeros((4, 512), F32)
    gather = (iota((512, 128), 0) // 8 == iota((512, 128), 1)).astype(F32)
    packed = jnp.dot(gm[...], gather, preferred_element_type=F32, precision=lax.Precision.HIGHEST)
    ar[0, 0:16, :] = packed[0:16] + swap(packed[24:40])
    ar[0, 16:24, :] = packed[16:24]

    def reduce_copies(axis):
        return [
            pltpu.make_async_remote_copy(
                src_ref=ar.at[axis], dst_ref=ar_in.at[axis, me[axis]],
                send_sem=ar_send.at[axis, step], recv_sem=ar_recv.at[axis, step],
                device_id=peer(axis, step), device_id_type=MESH,
            )
            for step in range(1, sizes[axis])
        ]

    def reduce_start(axis):
        copies = reduce_copies(axis)
        for copy in copies:
            copy.start()
        ar_in[axis, me[axis]] = ar[axis]
        return copies

    def reduce_end(axis, copies):
        for copy in copies:
            copy.wait_recv()
        total = ar_in[axis, 0]
        for rank in range(1, sizes[axis]):
            total = total + ar_in[axis, rank]
        ar[axis + 1] = total

    def physics(cell, base, comp):
        u = [vv[cell, base + v] for v in range(5)]
        inverse = recip(u[0])
        speed = u[1 + comp] * inverse
        square = u[1] * u[1] + u[2] * u[2] + u[3] * u[3]
        pressure = 0.4 * (u[4] - 0.5 * square * inverse)
        return u, inverse, speed, square, pressure

    def split_flux(c0, count, base, comp):
        def step(c, carry):
            cell = c0 + c
            u, _, speed, _, pressure = physics(cell, base, comp)
            flux = [u[1 + comp]] + [u[1 + k] * speed for k in range(3)] + [(u[4] + pressure) * speed]
            flux[1 + comp] = flux[1 + comp] + pressure
            for v in range(5):
                part = 0.5 * flux[v]
                wave = 2.0 * u[v]
                fp[cell, base + v] = part + wave
                fm[cell, base + v] = part - wave
            return carry

        lax.fori_loop(0, count, step, 0)

    def pull_flux(c0, count, base, comp):
        def step(c, carry):
            cell = c0 + c
            u, inverse, speed, square, pressure = physics(cell, base, comp)
            plus = [dfp[cell, base + v] for v in range(5)]
            minus = [dfm[cell, base + v] for v in range(5)]
            df = [0.5 * (a + b) for a, b in zip(plus, minus)]
            du = [2.0 * (a - b) for a, b in zip(plus, minus)]
            d_speed = df[4] * (u[4] + pressure)
            for k in range(3):
                d_speed = d_speed + df[1 + k] * u[1 + k]
            d_energy = df[4] * speed
            d_press = 0.4 * (df[1 + comp] + d_energy)
            slope = d_press * inverse
            du[4] = du[4] + d_energy + d_press
            for k in range(3):
                du[1 + k] = du[1 + k] + df[1 + k] * speed - slope * u[1 + k]
            du[1 + comp] = du[1 + comp] + df[0] + d_speed * inverse
            d_inverse = d_speed * u[1 + comp] - 0.5 * square * d_press
            du[0] = du[0] - inverse * inverse * d_inverse
            for v in range(5):
                dv[cell, base + v] += du[v]
            return carry

        lax.fori_loop(0, count, step, 0)

    def weno(c0, l0, p0, r0, faces, first, last):
        def step(q, carry):
            plus = [fp[c0 + c, q] for c in range(faces + 4)]
            minus = [fm[c0 + c, q] for c in range(faces + 4, 0, -1)]
            lam = [ll[l0 + k, q] for k in range(faces + 1)]
            cots = [lam[k + 1] - lam[k] for k in range(faces)]
            value_p, d_plus = line_weno(plus, cots)
            value_m, d_minus = line_weno(minus, cots[::-1])
            flux = [value_p[k] + value_m[faces - 1 - k] + corr_s[p0 + k, q] for k in range(faces)]
            for c in range(faces - 1):
                res_s[r0 + c, q] = flux[c] - flux[c + 1]
            for c in range(faces + 4):
                dfp[c0 + c, q] = d_plus[c]
                dfm[c0 + faces + 4 - c, q] = d_minus[c]
            dfp[c0 + faces + 4, q] = jnp.zeros((8, 128), F32)
            dfm[c0, q] = jnp.zeros((8, 128), F32)
            return carry

        lax.fori_loop(first, last, step, 0)

    def back(src, dst, index, axis, step):
        return remote(src, dst, back_send, back_recv, index, axis, step)

    waiting = reduce_start(0)
    started = list(waiting)

    split_flux(XC, 10, 0, 0)
    split_flux(XC, 10, 5, 0)
    weno(XC, 10, 9, 8, 5, 0, 10)
    pull_flux(XC, 10, 0, 0)
    pull_flux(XC, 10, 5, 0)
    back_x = [back(dv.at[XC : XC + 3], xbr.at[1], 0, 0, -1), back(dv.at[XC + 7 : XC + 10], xbr.at[0], 1, 0, 1)]
    for copy in back_x:
        copy.start()

    reduce_end(0, waiting)
    waiting = reduce_start(1)
    started += waiting

    split_flux(0, 14, 5, 2)
    weno(0, 0, 0, 0, 9, 5, 10)
    pull_flux(0, 14, 5, 2)
    for v in range(5):
        for r in range(8):
            zw[v, pl.ds(r, 8, stride=8), :] = dv[r, 5 + v]
            zl[v, pl.ds(r, 8, stride=8), :] = res_s[r, 5 + v]
        zw[v, 64:72, :] = jnp.zeros((8, 128), F32)
        for r in range(8, 14):
            zw[v, pl.ds(r, 8, stride=8), :] += dv[r, 5 + v]
        zb[0, 3 * v : 3 * v + 3, :] = zw[v, 0:3, :]
        zb[1, 3 * v : 3 * v + 3, :] = zw[v, 67:70, :]
    back_z = [back(zb.at[0], zbr.at[1], 4, 2, -1), back(zb.at[1], zbr.at[0], 5, 2, 1)]
    for copy in back_z:
        copy.start()

    reduce_end(1, waiting)
    waiting = reduce_start(2)
    started += waiting

    split_flux(0, 14, 0, 1)
    weno(0, 0, 0, 0, 9, 0, 5)
    pull_flux(0, 14, 0, 1)
    for v in range(5):
        for j in range(3):
            at = (3 * v + j) * 4
            yb[0, at : at + 4, :] = dv[j, v, 0:4, :]
            yb[1, at : at + 4, :] = dv[11 + j, v, 4:8, :]
    back_y = [back(yb.at[0], ybr.at[1], 2, 1, -1), back(yb.at[1], ybr.at[0], 3, 1, 1)]
    for copy in back_y:
        copy.start()

    for copy in back_z:
        copy.wait_recv()
    for v in range(5):
        near = zw[v, 0:3, :]
        far = zw[v, 67:70, :]
        zw[v, 64:67, :] += swap(jnp.where(low3, zbr[1, 3 * v : 3 * v + 3, :], near))
        zw[v, 3:6, :] += swap(jnp.where(low3, far, zbr[0, 3 * v : 3 * v + 3, :]))
    fields = [(zw, adj_o, 3, v) for v in range(5)] + [(zl, res_o, 0, v) for v in range(5)]
    for first, second in zip(fields[0::2], fields[1::2]):
        one = first[0][first[3], first[2] : first[2] + 64, :]
        two = second[0][second[3], second[2] : second[2] + 64, :]
        upper = jnp.where(low, one, swap(two))
        lower = jnp.where(low, swap(one), two)
        turned = jnp.transpose(jnp.concatenate([upper, lower], axis=0))
        first[1][first[3]] = turned[0:64]
        second[1][second[3]] = turned[64:128]

    for copy in back_x:
        copy.wait_recv()
    for v in range(5):
        for i in range(4):
            for t in range(2):
                at = i * 16 + t * 8
                value = dv[XC + 3 + i, 5 * t + v]
                if i < 3:
                    value = value + xbr[0, i, 5 * t + v]
                if i > 0:
                    value = value + xbr[1, i - 1, 5 * t + v]
                adj_o[v, at : at + 8, :] += value
                res_o[v, at : at + 8, :] += res_s[8 + i, 5 * t + v]

    for v in range(5):
        for r in range(14):
            for h in range(2):
                y = 8 * h + r - 3
                if 0 <= y < 16:
                    adj_o[v, pl.ds(y, 4, stride=16), :] += dv[r, v, 4 * h : 4 * h + 4, :]
        for j in range(8):
            for h in range(2):
                res_o[v, pl.ds(8 * h + j, 4, stride=16), :] += res_s[j, v, 4 * h : 4 * h + 4, :]
    for copy in back_y:
        copy.wait_recv()
    for v in range(5):
        for j in range(3):
            at = (3 * v + j) * 4
            adj_o[v, pl.ds(j, 4, stride=16), :] += ybr[0, at : at + 4, :]
            adj_o[v, pl.ds(13 + j, 4, stride=16), :] += ybr[1, at : at + 4, :]

    reduce_end(2, waiting)
    gwi_o[...] = jnp.transpose(jnp.concatenate([ar[3], swap(ar[3, 0:8, :])], axis=0))[0:64, 0:30]
    gm[0:16, 0:128] = swap(ar[3, 0:16, :])
    gbi_o[...] = gm[6:7, 0:64]
    gwo_o[...] = gm[7:12, 0:64]

    for copy in halo + started + back_x + back_y + back_z:
        copy.wait_send()


def per_device(density, momentum, energy, cotangent, w_in, b_in, w_out):
    sizes = tuple(lax.axis_size(a) for a in AXES)
    most = max(sizes)
    vmem = pl.BlockSpec(memory_space=pltpu.VMEM)
    tiles = lambda n: pltpu.VMEM((n, 10, 8, 128), F32)
    dma = pltpu.SemaphoreType.DMA
    out = pl.pallas_call(
        functools.partial(kernel, sizes),
        out_shape=(
            jax.ShapeDtypeStruct((5, 64, 128), F32),
            jax.ShapeDtypeStruct((5, 64, 128), F32),
            jax.ShapeDtypeStruct((64, 30), F32),
            jax.ShapeDtypeStruct((1, 64), F32),
            jax.ShapeDtypeStruct((5, 64), F32),
        ),
        in_specs=[vmem] * 7,
        out_specs=(vmem,) * 5,
        scratch_shapes=[
            pltpu.VMEM((5, 64, 128), F32), pltpu.VMEM((5, 64, 128), F32),
            tiles(24), tiles(16), tiles(24), tiles(24), tiles(24), tiles(24), tiles(24), tiles(14), tiles(12),
            pltpu.VMEM((5, 72, 128), F32), pltpu.VMEM((5, 64, 128), F32),
            pltpu.VMEM((512, 256), BF16), pltpu.VMEM((240, 512), BF16),
            pltpu.VMEM((48, 512), BF16), pltpu.VMEM((512, 48), BF16),
            pltpu.VMEM((512, 256), BF16), pltpu.VMEM((512, 256), BF16),
            pltpu.VMEM((256, 512), F32), pltpu.VMEM((48, 512), F32), pltpu.VMEM((40, 512), F32),
            pltpu.VMEM((4, 24, 128), F32), pltpu.VMEM((3, most, 24, 128), F32),
            pltpu.VMEM((2, 64, 128), F32), pltpu.VMEM((2, 64, 128), F32),
            pltpu.VMEM((2, 16, 128), F32), pltpu.VMEM((2, 16, 128), F32),
            pltpu.VMEM((2, 5, 48, 128), F32),
            pltpu.VMEM((2, 64, 128), F32), pltpu.VMEM((2, 64, 128), F32),
            pltpu.VMEM((2, 16, 128), F32), pltpu.VMEM((2, 16, 128), F32),
            pltpu.VMEM((2, 3, 10, 8, 128), F32),
            dma((6,)), dma((6,)), dma((6,)), dma((6,)), dma((3, most)), dma((3, most)),
        ],
        compiler_params=pltpu.CompilerParams(
            collective_id=0, has_side_effects=True, vmem_limit_bytes=40 * 1024 * 1024
        ),
        name="section",
    )(
        density.reshape(64, 128), momentum.reshape(3, 64, 128), energy.reshape(64, 128),
        cotangent.reshape(5, 64, 128), w_in, b_in[None, :], w_out,
    )
    residual, adjoint, grad_w_in, grad_b_in, grad_w_out = out
    return (
        residual.reshape(5, 4, 16, 128), adjoint.reshape(5, 4, 16, 128),
        grad_w_in, grad_b_in[0], grad_w_out,
    )


def solution(mesh):
    return jax.shard_map(
        per_device,
        mesh=mesh,
        in_specs=(
            P("gx", "gy", "gz"),
            P(None, "gx", "gy", "gz"),
            P("gx", "gy", "gz"),
            P(None, "gx", "gy", "gz"),
            P(),
            P(),
            P(),
        ),
        out_specs=(P(None, "gx", "gy", "gz"), P(None, "gx", "gy", "gz"), P(), P(), P()),
        check_vma=False,
    )
```

time: 389 us -> 52.3 us (0.13)
  blocking collectives: 99.1 us -> 0 us
  other arithmetic: 88.7 us -> 0 us
  local copies, waits for them, and re-layouts: 86.4 us -> 7.15 us
  matrix products: 52 us -> 0 us
  starting transfers between devices: 47.6 us -> 0 us
  Pallas kernels: 0 us -> 44.1 us
  loops' own time: 5.39 us -> 0 us
  waiting for transfers between devices: 4.61 us -> 0 us
    psum x1 -> x0, blocking collectives: 99.1 us -> none  [per_device(): lax.psum((local_w_in, local_b_in, local_w_out), ('gx', 'gy', 'gz'))]
    dot_general x72 -> x0, matrix products: 52 us -> none  [product(): return jnp.dot(left, right, preferred_element_type=jnp.float32)]
    ppermute x12 -> x0, starting transfers between devices: 47.6 us -> none  [the longest x6 26.2 us: with_halo(): after = lax.ppermute(leading, axis, down)]
    pallas_call x0 -> x1, Pallas kernels: none -> 44.1 us  [per_device(): pl.pallas_call(functools.partial(kernel, sizes), out_shape=(jax.ShapeDtyp...]
    add_any x188 -> x0, other arithmetic: 39.3 us -> none  [the longest x42 25.8 us: front(): plus = [0.5 * (f + ALPHA * c) for f, c in zip(fluxes, cells)]]
    while x429 -> x0, local copies, waits for them, and re-layouts: 26.2 us -> none
    concatenate x84 -> x0, local copies, waits for them, and re-layouts: 16.3 us -> none  [front(): return (weno, jnp.concatenate(cells, axis=0))]
    split x84 -> x0, local copies, waits for them, and re-layouts: 15.1 us -> none  [front(): return (weno, jnp.concatenate(cells, axis=0))]
  transfers between devices with their start and end apart: 12 -> 0, of which waited for: 1 -> 0; matrix products, arithmetic and copies ran while one was open for 52% -> 0% of each run, Pallas kernels for 0% -> 0%
where the time goes in v1:
time: 52.3 us; the launch traced here: 52 us
  Pallas kernels  44.1 us (84%)
  local copies, waits for them, and re-layouts  7.15 us (14%)
  between operations  0.68 us (1%)
    pallas_call x1, Pallas kernels, per_device(): pl.pallas_call(functools.partial(kernel, sizes), out_shape=(jax.ShapeDtyp...  44.1 us
    unnamed x18, local copies, waits for them, and re-layouts  7.15 us

profile of v1, /device:TPU:1, one launch (start us, length us, event | category | flops | bytes accessed | tf_op | source)
XLA Modules:
  0.0 52.0 jit_solution(13460807740749682566)
XLA Ops:
  0.6 0.0 copy-start.2
  0.6 0.0 copy-start.5
  0.7 0.8 %copy.12.w_in = bf16[64,30]{1,0:T(8,128)(2,1)S(1)} copy(bf16[64,30]{0,1:T(8,128)(2,1)} %param.11) | data formatting | bytes 7680 | tf_op args[4]
  1.5 0.0 copy-done.2
  1.5 0.0 copy-done.5
  1.5 0.0 copy-start
  1.5 0.9 %copy-done = f32[3,4,16,128]{3,2,1,0:T(8,128)S(1)} copy-done((f32[3,4,16,128]{3,2,1,0:T(8,128)S(1)}, f32[3,4,16,128]{3,2,1,0:T(8,128)}, u32[]{:S(2)}) %copy-start) | copy-done | bytes 98328
  2.4 0.0 copy-start.1
  2.4 0.9 %copy-done.1 = bf16[5,4,16,128]{3,2,1,0:T(8,128)(2,1)S(1)} copy-done((bf16[5,4,16,128]{3,2,1,0:T(8,128)(2,1)S(1)}, bf16[5,4,16,128]{3,2,1,0:T(8,128)(2,1)}, u32[]{:S(2)}) %copy-start.1) | copy-done | bytes 81944
  3.3 0.0 copy-start.3
  3.3 0.8 %copy-done.3 = f32[4,16,128]{2,1,0:T(8,128)S(1)} copy-done((f32[4,16,128]{2,1,0:T(8,128)S(1)}, f32[4,16,128]{2,1,0:T(8,128)}, u32[]{:S(2)}) %copy-start.3) | copy-done | bytes 32792
  4.0 0.0 copy-start.4
  4.0 0.7 %copy-done.4 = bf16[5,64]{1,0:T(8,128)(2,1)S(1)} copy-done((bf16[5,64]{1,0:T(8,128)(2,1)S(1)}, bf16[5,64]{1,0:T(8,128)(2,1)}, u32[]{:S(2)}) %copy-start.4) | copy-done | bytes 664
  4.7 44.1 %section.1 = (f32[5,64,128]{2,1,0:T(8,128)S(1)}, f32[5,64,128]{2,1,0:T(8,128)S(1)}, f32[64,30]{1,0:T(8,128)S(1)}, f32[1,64]{1,0:T(1,128)S(1)}, f32[5,64]{1,0:T(8,128)S(1)}) custom-call(f32[64,128]{1,0:T(8,128)S(1)} %bitcast.12, f32[3,64,128]{2,1,0:T(8,128)S(1)} %bitcast.10, f32[64,128]{1,0:T(8,128)S(1)} %bitcast.13, bf16[5,64,128]{2,1,0:T(8,128)(2,1)S(1)} %bitcast.11, ...), custom_call_target="tpu_custom_call" | custom-call | tf_op jit(solution)/shard_map/section/pallas_call | solution.py:494
  48.8 0.7 %copy.13 = f32[64,30]{0,1:T(8,128)} copy(f32[64,30]{1,0:T(8,128)S(1)} %get-tuple-element.17) | data formatting | bytes 15360
  49.5 0.7 %copy.18 = f32[5,4,16,128]{3,2,1,0:T(8,128)} copy(f32[5,4,16,128]{3,2,1,0:T(8,128)S(1)} %bitcast.9) | data formatting | bytes 327680
  50.2 0.7 %copy.19 = f32[5,4,16,128]{3,2,1,0:T(8,128)} copy(f32[5,4,16,128]{3,2,1,0:T(8,128)S(1)} %bitcast.8) | data formatting | bytes 327680
  50.9 0.5 copy.20
  51.4 0.6 %copy.21 = f32[5,64]{1,0:T(8,128)} copy(f32[5,64]{1,0:T(8,128)S(1)} %get-tuple-element.29) | data formatting | bytes 2560
Async XLA Ops:
  0.6 0.8 %copy-start.2 = (f32[4,16,128]{2,1,0:T(8,128)S(1)}, f32[4,16,128]{2,1,0:T(8,128)}, u32[]{:S(2)}) copy-start(f32[4,16,128]{2,1,0:T(8,128)} %param.7) | copy-start | bytes 98308
  0.6 0.8 %copy-start.5 = (f32[64]{0:T(128)S(1)}, f32[64]{0:T(128)}, u32[]{:S(2)}) copy-start(f32[64]{0:T(128)} %param.12) | copy-start | bytes 772
  1.5 0.9 %copy-start = (f32[3,4,16,128]{3,2,1,0:T(8,128)S(1)}, f32[3,4,16,128]{3,2,1,0:T(8,128)}, u32[]{:S(2)}) copy-start(f32[3,4,16,128]{3,2,1,0:T(8,128)} %param.8) | copy-start | bytes 294916
  2.4 0.9 %copy-start.1 = (bf16[5,4,16,128]{3,2,1,0:T(8,128)(2,1)S(1)}, bf16[5,4,16,128]{3,2,1,0:T(8,128)(2,1)}, u32[]{:S(2)}) copy-start(bf16[5,4,16,128]{3,2,1,0:T(8,128)(2,1)} %param.10) | copy-start | bytes 245764
  3.3 0.8 %copy-start.3 = (f32[4,16,128]{2,1,0:T(8,128)S(1)}, f32[4,16,128]{2,1,0:T(8,128)}, u32[]{:S(2)}) copy-start(f32[4,16,128]{2,1,0:T(8,128)} %param.9) | copy-start | bytes 98308
  4.0 0.7 %copy-start.4 = (bf16[5,64]{1,0:T(8,128)(2,1)S(1)}, bf16[5,64]{1,0:T(8,128)(2,1)}, u32[]{:S(2)}) copy-start(bf16[5,64]{1,0:T(8,128)(2,1)} %w_out.1) | copy-start | bytes 1924

commit v2 on v1

--- a/solution.py
+++ b/solution.py
@@ -102,12 +102,12 @@
 
 
 def kernel(
-    sizes, dens, mom, ener, cot, w_in, b_in, w_out,
-    res_o, adj_o, gwi_o, gbi_o, gwo_o,
-    nat, lamn, vv, ll, fp, fm, dfp, dfm, dv, corr_s, res_s,
+    sizes, dens, mom, ener, cot, w_in_h, b_in_h, w_out_h,
+    res_o, adj_o, grad_o,
+    cotv, w_in, b_in, w_out, fea, dco, nat, lamn, vv, ll, fp, fm, dfp, dfm, dv, corr_s, res_s,
     zw, zl, w1, w1t, w2, w2t, hid, dpr, g1, g2, gm, ar, ar_in,
     ys, yr, zs, zr, xr, yb, ybr, zb, zbr, xbr,
-    halo_send, halo_recv, back_send, back_recv, ar_send, ar_recv,
+    halo_send, halo_recv, back_send, back_recv, ar_send, ar_recv, load_sem,
 ):
     me = [lax.axis_index(a) for a in AXES]
 
@@ -120,15 +120,24 @@
         for step in range(1, sizes[axis]):
             pl.semaphore_signal(bar, 1, device_id=peer(axis, step), device_id_type=MESH)
 
+    loads = [
+        pltpu.make_async_copy(src, dst, load_sem.at[index])
+        for index, (src, dst) in enumerate((
+            (dens, nat.at[0]), (mom, nat.at[1:4]), (ener, nat.at[4]), (cot, cotv),
+            (w_in_h, w_in), (b_in_h, b_in), (w_out_h, w_out),
+        ))
+    ]
+    for copy in loads:
+        copy.start()
+
     lane = lax.broadcasted_iota(jnp.int32, (64, 128), 1)
     low = lane < 64
     lane8 = lax.broadcasted_iota(jnp.int32, (3, 128), 1)
     low3 = lane8 < 64
 
-    nat[0] = dens[...]
-    nat[1:4] = mom[...]
-    nat[4] = ener[...]
-    lamn[...] = cot[...].astype(F32)
+    for copy in loads:
+        copy.wait()
+    lamn[...] = cotv[...].astype(F32)
 
     def swap(value):
         return pltpu.roll(value, 64, 1)
@@ -184,11 +193,10 @@
     bias_c = bias - bias_a - bias_b
     row = iota((256, 64), 0)
     bias_rows = jnp.where(row == 240, bias_a, jnp.where(row == 241, bias_b, jnp.where(row == 242, bias_c, 0.0)))
-    wide_in = dot(w_in[...], one_hot((30, 256), 1)).astype(BF16)
-    full_in = jnp.where(same_row((512, 256)), dot(spread, wide_in), 0.0)
-    w1[...] = (full_in + dot_nt(spread, bias_rows.astype(BF16))).astype(BF16)
-    tall_in = dot_nt(one_hot((240, 30), 0), w_in[...]).astype(BF16)
-    w1t[...] = jnp.where(same_row((240, 512)), dot(tall_in, spread_t), 0.0).astype(BF16)
+    tall_in = (dot(one_hot((256, 30), 0), w_in[...]) + bias_rows).astype(BF16)
+    kept = same_row((512, 256)) | (iota((512, 256), 1) >= 240)
+    w1[...] = jnp.where(kept, dot_nt(spread, tall_in), 0.0).astype(BF16)
+    w1t[...] = jnp.where(same_row((240, 512)), dot(tall_in[0:240], spread_t), 0.0).astype(BF16)
     tall_out = dot(one_hot((48, 5), 0), w_out[...]).astype(BF16)
     w2[...] = jnp.where(same_row((48, 512)), dot(tall_out, spread_t), 0.0).astype(BF16)
     wide_out = dot_nt(spread, w_out[...]).astype(BF16)
@@ -216,6 +224,44 @@
     g1[...] = jnp.zeros(g1.shape, F32)
     g2[...] = jnp.zeros(g2.shape, F32)
 
+    ones = jnp.ones((16, 256), BF16)
+    blank = jnp.zeros((8, 256), F32)
+
+    def network(p0, c0, l0, count):
+        for f in range(count):
+            cells = [vv[pl.ds(c0 + f, 6), 5 * t : 5 * t + 5].reshape(240, 128) for t in range(2)]
+            feats = jnp.concatenate([jnp.concatenate(cells, axis=1).astype(BF16), ones], axis=0)
+            steps = [
+                (ll[l0 + f + 1, 5 * t : 5 * t + 5] - ll[l0 + f, 5 * t : 5 * t + 5]).reshape(40, 128) for t in range(2)
+            ]
+            dcorr = jnp.concatenate([jnp.concatenate(steps, axis=1), blank], axis=0).astype(BF16)
+            lanes = slice(256 * f, 256 * f + 256)
+            fea[:, lanes] = feats
+            dco[:, lanes] = dcorr
+            for part in range(4):
+                rows = slice(128 * part, 128 * part + 128)
+                act = jnp.tanh(dot(w1[rows, :], feats))
+                hid[rows, lanes] = act.astype(BF16)
+                dpr[rows, lanes] = (dot(w2t[rows, :], dcorr) * (1.0 - act * act)).astype(BF16)
+        wide = slice(0, 256 * count)
+        total = {}
+        for f in range(count):
+            lanes = slice(256 * f, 256 * f + 256)
+            corr = dot(w2[...], hid[:, lanes])
+            dfeat = dot(w1t[...], dpr[:, lanes])
+            for t in range(2):
+                tile = slice(128 * t, 128 * t + 128)
+                corr_s[p0 + f, 5 * t : 5 * t + 5] = corr[0:40, tile].reshape(5, 8, 128)
+                for c in range(6):
+                    part = dfeat[40 * c : 40 * c + 40, tile].reshape(5, 8, 128)
+                    total[f + c, t] = part if (f + c, t) not in total else total[f + c, t] + part
+        for (c, t), part in total.items():
+            dv[c0 + c, 5 * t : 5 * t + 5] += part
+        g1[...] += dot_nt(fea[:, wide], dpr[:, wide])
+        g2[...] += dot_nt(dco[:, wide], hid[:, wide])
+
+    network(3, 3, 3, 3)
+
     for copy in halo[2:]:
         copy.wait_recv()
     for v in range(5):
@@ -228,33 +274,11 @@
         for r in (0, 1, 2, 11, 12, 13):
             vv[r, 5 + v] = zw[v, pl.ds(r, 8, stride=8), :]
 
-    ones = jnp.ones((16, 256), BF16)
-    blank = jnp.zeros((8, 256), F32)
-
-    def network(p, c0, lb):
-        cells = [vv[pl.ds(c0, 6), 5 * t : 5 * t + 5].reshape(240, 128) for t in range(2)]
-        feats = jnp.concatenate([jnp.concatenate(cells, axis=1).astype(BF16), ones], axis=0)
-        steps = [(ll[lb + 1, 5 * t : 5 * t + 5] - ll[lb, 5 * t : 5 * t + 5]).reshape(40, 128) for t in range(2)]
-        dcorr = jnp.concatenate([jnp.concatenate(steps, axis=1), blank], axis=0).astype(BF16)
-        for part in range(4):
-            rows = pl.ds(128 * part, 128)
-            act = jnp.tanh(dot(w1[rows, :], feats))
-            hid[rows, :] = act.astype(BF16)
-            dpr[rows, :] = (dot(w2t[rows, :], dcorr) * (1.0 - act * act)).astype(BF16)
-        corr = dot(w2[...], hid[...])
-        dfeat = dot(w1t[...], dpr[...])
-        for t in range(2):
-            lanes = slice(128 * t, 128 * t + 128)
-            corr_s[p, 5 * t : 5 * t + 5] = corr[0:40, lanes].reshape(5, 8, 128)
-            dv[pl.ds(c0, 6), 5 * t : 5 * t + 5] += dfeat[:, lanes].reshape(6, 5, 8, 128)
-        g1[...] += dot_nt(feats, dpr[...])
-        g2[...] += dot_nt(dcorr, hid[...])
-
-    def net_yz(p, carry):
-        network(p, p, p)
+    def net_yz(i, carry):
+        network(6 * i, 6 * i, 6 * i, 3)
         return carry
 
-    lax.fori_loop(0, 9, net_yz, 0)
+    lax.fori_loop(0, 2, net_yz, 0)
 
     for copy in halo[:2]:
         copy.wait_recv()
@@ -264,12 +288,7 @@
                 at = i * 16 + t * 8
                 vv[XC + i, 5 * t + v] = xr[0, v, at : at + 8, :]
                 vv[XC + 7 + i, 5 * t + v] = xr[1, v, at : at + 8, :]
-
-    def net_x(k, carry):
-        network(9 + k, XC + k, 10 + k)
-        return carry
-
-    lax.fori_loop(0, 5, net_x, 0)
+    network(9, XC, 10, 5)
 
     inner = jnp.where(same_row((240, 512)), g1[0:240, :], 0.0).reshape(30, 8, 512)
     outer = jnp.where(same_row((40, 512)), g2[0:40, :], 0.0).reshape(5, 8, 512)
@@ -282,30 +301,30 @@
     ar[0, 0:16, :] = packed[0:16] + swap(packed[24:40])
     ar[0, 16:24, :] = packed[16:24]
 
-    def reduce_copies(axis):
-        return [
+    order = (2, 1, 0)
+
+    def reduce_start(phase):
+        axis = order[phase]
+        copies = [
             pltpu.make_async_remote_copy(
-                src_ref=ar.at[axis], dst_ref=ar_in.at[axis, me[axis]],
-                send_sem=ar_send.at[axis, step], recv_sem=ar_recv.at[axis, step],
+                src_ref=ar.at[phase], dst_ref=ar_in.at[phase, me[axis]],
+                send_sem=ar_send.at[phase, step], recv_sem=ar_recv.at[phase, step],
                 device_id=peer(axis, step), device_id_type=MESH,
             )
             for step in range(1, sizes[axis])
         ]
-
-    def reduce_start(axis):
-        copies = reduce_copies(axis)
         for copy in copies:
             copy.start()
-        ar_in[axis, me[axis]] = ar[axis]
+        ar_in[phase, me[axis]] = ar[phase]
         return copies
 
-    def reduce_end(axis, copies):
+    def reduce_end(phase, copies):
         for copy in copies:
             copy.wait_recv()
-        total = ar_in[axis, 0]
-        for rank in range(1, sizes[axis]):
-            total = total + ar_in[axis, rank]
-        ar[axis + 1] = total
+        total = ar_in[phase, 0]
+        for rank in range(1, sizes[order[phase]]):
+            total = total + ar_in[phase, rank]
+        ar[phase + 1] = total
 
     def physics(cell, base, comp):
         u = [vv[cell, base + v] for v in range(5)]
@@ -328,7 +347,7 @@
                 fm[cell, base + v] = part - wave
             return carry
 
-        lax.fori_loop(0, count, step, 0)
+        lax.fori_loop(0, count, step, 0, unroll=count // 2)
 
     def pull_flux(c0, count, base, comp):
         def step(c, carry):
@@ -354,7 +373,7 @@
                 dv[cell, base + v] += du[v]
             return carry
 
-        lax.fori_loop(0, count, step, 0)
+        lax.fori_loop(0, count, step, 0, unroll=count // 2)
 
     def weno(c0, l0, p0, r0, faces, first, last):
         def step(q, carry):
@@ -476,39 +495,48 @@
             adj_o[v, pl.ds(13 + j, 4, stride=16), :] += ybr[1, at : at + 4, :]
 
     reduce_end(2, waiting)
-    gwi_o[...] = jnp.transpose(jnp.concatenate([ar[3], swap(ar[3, 0:8, :])], axis=0))[0:64, 0:30]
-    gm[0:16, 0:128] = swap(ar[3, 0:16, :])
-    gbi_o[...] = gm[6:7, 0:64]
-    gwo_o[...] = gm[7:12, 0:64]
+    grad_o[0:24, :] = ar[3]
+    grad_o[24:40, :] = swap(ar[3, 0:16, :])
 
     for copy in halo + started + back_x + back_y + back_z:
         copy.wait_send()
+
+
+def finish(res, adj, grad, res_h, adj_h, gwi_h, gbi_h, gwo_h, gwi, gbi, gwo, sems):
+    gwi[...] = grad[0:30, 0:64]
+    gbi[...] = grad[30:31, 0:64]
+    gwo[...] = grad[31:36, 0:64]
+    pairs = ((res, res_h), (adj, adj_h), (gwi, gwi_h), (gbi, gbi_h), (gwo, gwo_h))
+    copies = [pltpu.make_async_copy(src, dst, sems.at[index]) for index, (src, dst) in enumerate(pairs)]
+    for copy in copies:
+        copy.start()
+    for copy in copies:
+        copy.wait()
 
 
 def per_device(density, momentum, energy, cotangent, w_in, b_in, w_out):
     sizes = tuple(lax.axis_size(a) for a in AXES)
     most = max(sizes)
     vmem = pl.BlockSpec(memory_space=pltpu.VMEM)
+    hbm = pl.BlockSpec(memory_space=pltpu.HBM)
     tiles = lambda n: pltpu.VMEM((n, 10, 8, 128), F32)
     dma = pltpu.SemaphoreType.DMA
-    out = pl.pallas_call(
+    block = jax.ShapeDtypeStruct((5, 64, 128), F32)
+    residual, adjoint, grads = pl.pallas_call(
         functools.partial(kernel, sizes),
-        out_shape=(
-            jax.ShapeDtypeStruct((5, 64, 128), F32),
-            jax.ShapeDtypeStruct((5, 64, 128), F32),
-            jax.ShapeDtypeStruct((64, 30), F32),
-            jax.ShapeDtypeStruct((1, 64), F32),
-            jax.ShapeDtypeStruct((5, 64), F32),
-        ),
-        in_specs=[vmem] * 7,
-        out_specs=(vmem,) * 5,
+        out_shape=(block, block, jax.ShapeDtypeStruct((40, 128), F32)),
+        in_specs=[hbm] * 7,
+        out_specs=(vmem,) * 3,
         scratch_shapes=[
+            pltpu.VMEM((5, 64, 128), BF16), pltpu.VMEM((30, 64), BF16),
+            pltpu.VMEM((1, 64), F32), pltpu.VMEM((5, 64), BF16),
+            pltpu.VMEM((256, 1280), BF16), pltpu.VMEM((48, 1280), BF16),
             pltpu.VMEM((5, 64, 128), F32), pltpu.VMEM((5, 64, 128), F32),
             tiles(24), tiles(16), tiles(24), tiles(24), tiles(24), tiles(24), tiles(24), tiles(14), tiles(12),
             pltpu.VMEM((5, 72, 128), F32), pltpu.VMEM((5, 64, 128), F32),
             pltpu.VMEM((512, 256), BF16), pltpu.VMEM((240, 512), BF16),
             pltpu.VMEM((48, 512), BF16), pltpu.VMEM((512, 48), BF16),
-            pltpu.VMEM((512, 256), BF16), pltpu.VMEM((512, 256), BF16),
+            pltpu.VMEM((512, 1280), BF16), pltpu.VMEM((512, 1280), BF16),
             pltpu.VMEM((256, 512), F32), pltpu.VMEM((48, 512), F32), pltpu.VMEM((40, 512), F32),
             pltpu.VMEM((4, 24, 128), F32), pltpu.VMEM((3, most, 24, 128), F32),
             pltpu.VMEM((2, 64, 128), F32), pltpu.VMEM((2, 64, 128), F32),
@@ -517,20 +545,35 @@
             pltpu.VMEM((2, 64, 128), F32), pltpu.VMEM((2, 64, 128), F32),
             pltpu.VMEM((2, 16, 128), F32), pltpu.VMEM((2, 16, 128), F32),
             pltpu.VMEM((2, 3, 10, 8, 128), F32),
-            dma((6,)), dma((6,)), dma((6,)), dma((6,)), dma((3, most)), dma((3, most)),
+            dma((6,)), dma((6,)), dma((6,)), dma((6,)), dma((3, most)), dma((3, most)), dma((7,)),
         ],
         compiler_params=pltpu.CompilerParams(
             collective_id=0, has_side_effects=True, vmem_limit_bytes=40 * 1024 * 1024
         ),
         name="section",
     )(
-        density.reshape(64, 128), momentum.reshape(3, 64, 128), energy.reshape(64, 128),
-        cotangent.reshape(5, 64, 128), w_in, b_in[None, :], w_out,
+        *(pltpu.with_memory_space_constraint(a, pltpu.HBM) for a in (
+            density.reshape(64, 128), momentum.reshape(3, 64, 128), energy.reshape(64, 128),
+            cotangent.reshape(5, 64, 128), w_in.T, b_in[None, :], w_out,
+        ))
     )
-    residual, adjoint, grad_w_in, grad_b_in, grad_w_out = out
+    residual, adjoint, grad_w_in, grad_b_in, grad_w_out = pl.pallas_call(
+        finish,
+        out_shape=(
+            block, block,
+            jax.ShapeDtypeStruct((30, 64), F32), jax.ShapeDtypeStruct((1, 64), F32), jax.ShapeDtypeStruct((5, 64), F32),
+        ),
+        in_specs=[vmem] * 3,
+        out_specs=(hbm,) * 5,
+        scratch_shapes=[
+            pltpu.VMEM((30, 64), F32), pltpu.VMEM((1, 64), F32), pltpu.VMEM((5, 64), F32), dma((5,)),
+        ],
+        compiler_params=pltpu.CompilerParams(vmem_limit_bytes=16 * 1024 * 1024),
+        name="store",
+    )(residual, adjoint, grads)
     return (
         residual.reshape(5, 4, 16, 128), adjoint.reshape(5, 4, 16, 128),
-        grad_w_in, grad_b_in[0], grad_w_out,
+        grad_w_in.T, grad_b_in[0], grad_w_out,
     )
 
 

time: 52.3 us -> 39.9 us (0.76)
  local copies, waits for them, and re-layouts: 7.15 us -> 0 us
  Pallas kernels: 44.1 us -> 39.1 us
    unnamed x18 -> x0, local copies, waits for them, and re-layouts: 7.15 us -> none
    pallas_call x1 -> x2, Pallas kernels: 44.1 us -> 39.1 us  [the longest x1 38.3 us: per_device(): pl.pallas_call(functools.partial(kernel, sizes), out_shape=(block, block,...]
where the time goes in v2:
time: 39.9 us; the launch traced here: 39.8 us
  Pallas kernels  39.1 us (98%)
  between operations  0.64 us (2%)
    pallas_call x1, Pallas kernels, per_device(): pl.pallas_call(functools.partial(kernel, sizes), out_shape=(block, block,...  38.3 us

profile of v2, /device:TPU:1, one launch (start us, length us, event | category | flops | bytes accessed | tf_op | source)
XLA Modules:
  0.0 39.8 jit_solution(7615289174619245582)
XLA Ops:
  0.6 38.3 %section.1 = (f32[5,64,128]{2,1,0:T(8,128)S(1)}, f32[5,64,128]{2,1,0:T(8,128)S(1)}, f32[40,128]{1,0:T(8,128)S(1)}) custom-call(f32[64,128]{1,0:T(8,128)} %bitcast.12, f32[3,64,128]{2,1,0:T(8,128)} %bitcast.10, f32[64,128]{1,0:T(8,128)} %bitcast.13, bf16[5,64,128]{2,1,0:T(8,128)(2,1)} %bitcast.11, bf16[30,64]{1,0:T(8,128)(2,1)} %bitcast.14, ...), custom_call_target="tpu_custom_call" | custom-call | tf_op jit(solution)/shard_map/section/pallas_call | solution.py:525
  39.0 0.8 %store.1 = (f32[5,64,128]{2,1,0:T(8,128)}, f32[5,64,128]{2,1,0:T(8,128)}, f32[30,64]{1,0:T(8,128)}, f32[1,64]{1,0:T(1,128)}, f32[5,64]{1,0:T(8,128)}) custom-call(f32[5,64,128]{2,1,0:T(8,128)S(1)} %get-tuple-element.13.res, f32[5,64,128]{2,1,0:T(8,128)S(1)} %get-tuple-element.14.adj, f32[40,128]{1,0:T(8,128)S(1)} %get-tuple-element.15.grad), custom_call_target="tpu_custom_call" | custom-call | tf_op jit(solution)/shard_map/store/pallas_call | solution.py:560

commit v3 on v2

--- a/solution.py
+++ b/solution.py
@@ -107,7 +107,7 @@
     cotv, w_in, b_in, w_out, fea, dco, nat, lamn, vv, ll, fp, fm, dfp, dfm, dv, corr_s, res_s,
     zw, zl, w1, w1t, w2, w2t, hid, dpr, g1, g2, gm, ar, ar_in,
     ys, yr, zs, zr, xr, yb, ybr, zb, zbr, xbr,
-    halo_send, halo_recv, back_send, back_recv, ar_send, ar_recv, load_sem,
+    halo_send, halo_recv, back_send, back_recv, ar_send, ar_recv, load_sem, relay,
 ):
     me = [lax.axis_index(a) for a in AXES]
 
@@ -117,8 +117,18 @@
 
     bar = pltpu.get_barrier_semaphore()
     for axis in range(3):
-        for step in range(1, sizes[axis]):
+        for step in (-1, 1):
             pl.semaphore_signal(bar, 1, device_id=peer(axis, step), device_id_type=MESH)
+
+    def relay_send(turn):
+        for axis in range(3):
+            for side, step in enumerate((-1, 1)):
+                pl.semaphore_signal(relay.at[turn, axis, side], 1, device_id=peer(axis, step), device_id_type=MESH)
+
+    def relay_wait(turn):
+        for axis in range(3):
+            for side in range(2):
+                pl.semaphore_wait(relay.at[turn, axis, side], 1)
 
     loads = [
         pltpu.make_async_copy(src, dst, load_sem.at[index])
@@ -157,7 +167,7 @@
             ys[0, at : at + 4, :] = nat[v, pl.ds(j, 4, stride=16), :]
             ys[1, at : at + 4, :] = nat[v, pl.ds(13 + j, 4, stride=16), :]
 
-    pl.semaphore_wait(bar, sum(sizes) - 3)
+    pl.semaphore_wait(bar, 6)
 
     def remote(src, dst, send, recv, index, axis, step):
         return pltpu.make_async_remote_copy(
@@ -175,6 +185,7 @@
     ]
     for copy in halo:
         copy.start()
+    relay_send(0)
 
     def iota(shape, dim):
         return lax.broadcasted_iota(jnp.int32, shape, dim)
@@ -221,13 +232,15 @@
     for end in (0, 9, 10, 15):
         ll[end] = jnp.zeros((10, 8, 128), F32)
     dv[...] = jnp.zeros(dv.shape, F32)
-    g1[...] = jnp.zeros(g1.shape, F32)
-    g2[...] = jnp.zeros(g2.shape, F32)
 
     ones = jnp.ones((16, 256), BF16)
     blank = jnp.zeros((8, 256), F32)
 
-    def network(p0, c0, l0, count):
+    def tile_lanes(p):
+        return pl.ds(256 * p if isinstance(p, int) else pl.multiple_of(256 * p, 256), 256)
+
+    def network(p0, c0, l0, count, start=False):
+        lane0 = 256 * p0 if isinstance(p0, int) else pl.multiple_of(256 * p0, 256)
         for f in range(count):
             cells = [vv[pl.ds(c0 + f, 6), 5 * t : 5 * t + 5].reshape(240, 128) for t in range(2)]
             feats = jnp.concatenate([jnp.concatenate(cells, axis=1).astype(BF16), ones], axis=0)
@@ -235,7 +248,7 @@
                 (ll[l0 + f + 1, 5 * t : 5 * t + 5] - ll[l0 + f, 5 * t : 5 * t + 5]).reshape(40, 128) for t in range(2)
             ]
             dcorr = jnp.concatenate([jnp.concatenate(steps, axis=1), blank], axis=0).astype(BF16)
-            lanes = slice(256 * f, 256 * f + 256)
+            lanes = tile_lanes(p0 + f)
             fea[:, lanes] = feats
             dco[:, lanes] = dcorr
             for part in range(4):
@@ -243,10 +256,20 @@
                 act = jnp.tanh(dot(w1[rows, :], feats))
                 hid[rows, lanes] = act.astype(BF16)
                 dpr[rows, lanes] = (dot(w2t[rows, :], dcorr) * (1.0 - act * act)).astype(BF16)
-        wide = slice(0, 256 * count)
+        wide = pl.ds(lane0, 256 * count)
+        part1 = dot_nt(fea[:, wide], dpr[:, wide])
+        part2 = dot_nt(dco[:, wide], hid[:, wide])
+        if start:
+            g1[...] = part1
+            g2[...] = part2
+        else:
+            g1[...] += part1
+            g2[...] += part2
+
+    def products(p0, c0, count):
         total = {}
         for f in range(count):
-            lanes = slice(256 * f, 256 * f + 256)
+            lanes = tile_lanes(p0 + f)
             corr = dot(w2[...], hid[:, lanes])
             dfeat = dot(w1t[...], dpr[:, lanes])
             for t in range(2):
@@ -257,10 +280,10 @@
                     total[f + c, t] = part if (f + c, t) not in total else total[f + c, t] + part
         for (c, t), part in total.items():
             dv[c0 + c, 5 * t : 5 * t + 5] += part
-        g1[...] += dot_nt(fea[:, wide], dpr[:, wide])
-        g2[...] += dot_nt(dco[:, wide], hid[:, wide])
-
-    network(3, 3, 3, 3)
+
+    network(3, 3, 3, 3, start=True)
+    relay_wait(0)
+    relay_send(1)
 
     for copy in halo[2:]:
         copy.wait_recv()
@@ -279,6 +302,8 @@
         return carry
 
     lax.fori_loop(0, 2, net_yz, 0)
+    relay_wait(1)
+    relay_send(2)
 
     for copy in halo[:2]:
         copy.wait_recv()
@@ -298,8 +323,9 @@
     gm[36:40, :] = jnp.zeros((4, 512), F32)
     gather = (iota((512, 128), 0) // 8 == iota((512, 128), 1)).astype(F32)
     packed = jnp.dot(gm[...], gather, preferred_element_type=F32, precision=lax.Precision.HIGHEST)
-    ar[0, 0:16, :] = packed[0:16] + swap(packed[24:40])
-    ar[0, 16:24, :] = packed[16:24]
+    gm[:, 0:128] = packed
+    ar[0] = gm[0:18, 0:128] + swap(gm[18:36, 0:128])
+    relay_wait(2)
 
     order = (2, 1, 0)
 
@@ -401,6 +427,8 @@
     waiting = reduce_start(0)
     started = list(waiting)
 
+    products(9, XC, 5)
+
     split_flux(XC, 10, 0, 0)
     split_flux(XC, 10, 5, 0)
     weno(XC, 10, 9, 8, 5, 0, 10)
@@ -409,6 +437,12 @@
     back_x = [back(dv.at[XC : XC + 3], xbr.at[1], 0, 0, -1), back(dv.at[XC + 7 : XC + 10], xbr.at[0], 1, 0, 1)]
     for copy in back_x:
         copy.start()
+
+    def products_yz(i, carry):
+        products(3 * i, 3 * i, 3)
+        return carry
+
+    lax.fori_loop(0, 3, products_yz, 0)
 
     reduce_end(0, waiting)
     waiting = reduce_start(1)
@@ -429,10 +463,6 @@
     back_z = [back(zb.at[0], zbr.at[1], 4, 2, -1), back(zb.at[1], zbr.at[0], 5, 2, 1)]
     for copy in back_z:
         copy.start()
-
-    reduce_end(1, waiting)
-    waiting = reduce_start(2)
-    started += waiting
 
     split_flux(0, 14, 0, 1)
     weno(0, 0, 0, 0, 9, 0, 5)
@@ -463,6 +493,10 @@
         first[1][first[3]] = turned[0:64]
         second[1][second[3]] = turned[64:128]
 
+    reduce_end(1, waiting)
+    waiting = reduce_start(2)
+    started += waiting
+
     for copy in back_x:
         copy.wait_recv()
     for v in range(5):
@@ -495,8 +529,8 @@
             adj_o[v, pl.ds(13 + j, 4, stride=16), :] += ybr[1, at : at + 4, :]
 
     reduce_end(2, waiting)
-    grad_o[0:24, :] = ar[3]
-    grad_o[24:40, :] = swap(ar[3, 0:16, :])
+    grad_o[0:18, :] = ar[3]
+    grad_o[18:36, :] = swap(ar[3])
 
     for copy in halo + started + back_x + back_y + back_z:
         copy.wait_send()
@@ -530,15 +564,15 @@
         scratch_shapes=[
             pltpu.VMEM((5, 64, 128), BF16), pltpu.VMEM((30, 64), BF16),
             pltpu.VMEM((1, 64), F32), pltpu.VMEM((5, 64), BF16),
-            pltpu.VMEM((256, 1280), BF16), pltpu.VMEM((48, 1280), BF16),
+            pltpu.VMEM((256, 3584), BF16), pltpu.VMEM((48, 3584), BF16),
             pltpu.VMEM((5, 64, 128), F32), pltpu.VMEM((5, 64, 128), F32),
             tiles(24), tiles(16), tiles(24), tiles(24), tiles(24), tiles(24), tiles(24), tiles(14), tiles(12),
             pltpu.VMEM((5, 72, 128), F32), pltpu.VMEM((5, 64, 128), F32),
             pltpu.VMEM((512, 256), BF16), pltpu.VMEM((240, 512), BF16),
             pltpu.VMEM((48, 512), BF16), pltpu.VMEM((512, 48), BF16),
-            pltpu.VMEM((512, 1280), BF16), pltpu.VMEM((512, 1280), BF16),
+            pltpu.VMEM((512, 3584), BF16), pltpu.VMEM((512, 3584), BF16),
             pltpu.VMEM((256, 512), F32), pltpu.VMEM((48, 512), F32), pltpu.VMEM((40, 512), F32),
-            pltpu.VMEM((4, 24, 128), F32), pltpu.VMEM((3, most, 24, 128), F32),
+            pltpu.VMEM((4, 18, 128), F32), pltpu.VMEM((3, most, 18, 128), F32),
             pltpu.VMEM((2, 64, 128), F32), pltpu.VMEM((2, 64, 128), F32),
             pltpu.VMEM((2, 16, 128), F32), pltpu.VMEM((2, 16, 128), F32),
             pltpu.VMEM((2, 5, 48, 128), F32),
@@ -546,6 +580,7 @@
             pltpu.VMEM((2, 16, 128), F32), pltpu.VMEM((2, 16, 128), F32),
             pltpu.VMEM((2, 3, 10, 8, 128), F32),
             dma((6,)), dma((6,)), dma((6,)), dma((6,)), dma((3, most)), dma((3, most)), dma((7,)),
+            pltpu.SemaphoreType.REGULAR((3, 3, 2)),
         ],
         compiler_params=pltpu.CompilerParams(
             collective_id=0, has_side_effects=True, vmem_limit_bytes=40 * 1024 * 1024

time: 39.9 us -> 37.6 us (0.942)
  Pallas kernels: 39.1 us -> 36.8 us
    pallas_call x1, Pallas kernels: 38.3 us -> 36 us  [per_device(): pl.pallas_call(functools.partial(kernel, sizes), out_shape=(block, block,...]
where the time goes in v3:
time: 37.6 us; the launch traced here: 37.5 us
  Pallas kernels  36.8 us (98%)
  between operations  0.64 us (2%)
    pallas_call x1, Pallas kernels, per_device(): pl.pallas_call(functools.partial(kernel, sizes), out_shape=(block, block,...  36 us
    pallas_call x1, Pallas kernels, per_device(): pl.pallas_call(finish, out_shape=(block, block, jax.ShapeDtypeStruct((30,...  0.77 us

profile of v3, /device:TPU:1, one launch (start us, length us, event | category | flops | bytes accessed | tf_op | source)
XLA Modules:
  0.0 37.5 jit_solution(7644107447877894762)
XLA Ops:
  0.6 36.0 %section.1 = (f32[5,64,128]{2,1,0:T(8,128)S(1)}, f32[5,64,128]{2,1,0:T(8,128)S(1)}, f32[40,128]{1,0:T(8,128)S(1)}) custom-call(f32[64,128]{1,0:T(8,128)} %bitcast.12, f32[3,64,128]{2,1,0:T(8,128)} %bitcast.10, f32[64,128]{1,0:T(8,128)} %bitcast.13, bf16[5,64,128]{2,1,0:T(8,128)(2,1)} %bitcast.11, bf16[30,64]{1,0:T(8,128)(2,1)} %bitcast.14, ...), custom_call_target="tpu_custom_call" | custom-call | tf_op jit(solution)/shard_map/section/pallas_call | solution.py:559
  36.7 0.8 %store.1 = (f32[5,64,128]{2,1,0:T(8,128)}, f32[5,64,128]{2,1,0:T(8,128)}, f32[30,64]{1,0:T(8,128)}, f32[1,64]{1,0:T(1,128)}, f32[5,64]{1,0:T(8,128)}) custom-call(f32[5,64,128]{2,1,0:T(8,128)S(1)} %get-tuple-element.13.res, f32[5,64,128]{2,1,0:T(8,128)S(1)} %get-tuple-element.14.adj, f32[40,128]{1,0:T(8,128)S(1)} %get-tuple-element.15.grad), custom_call_target="tpu_custom_call" | custom-call | tf_op jit(solution)/shard_map/store/pallas_call | solution.py:595

commit v4 on v3

--- a/solution.py
+++ b/solution.py
@@ -301,9 +301,9 @@
         network(6 * i, 6 * i, 6 * i, 3)
         return carry
 
-    lax.fori_loop(0, 2, net_yz, 0)
     relay_wait(1)
     relay_send(2)
+    lax.fori_loop(0, 2, net_yz, 0)
 
     for copy in halo[:2]:
         copy.wait_recv()

time: 37.6 us -> 37.9 us (level)
  no operation moved by 1% of the time
where the time goes in v4:
time: 37.9 us; the launch traced here: 37.8 us
  Pallas kernels  37.1 us (98%)
  between operations  0.64 us (2%)
    pallas_call x1, Pallas kernels, per_device(): pl.pallas_call(functools.partial(kernel, sizes), out_shape=(block, block,...  36.4 us
    pallas_call x1, Pallas kernels, per_device(): pl.pallas_call(finish, out_shape=(block, block, jax.ShapeDtypeStruct((30,...  0.77 us

profile of v4, /device:TPU:1, one launch (start us, length us, event | category | flops | bytes accessed | tf_op | source)
XLA Modules:
  0.0 37.8 jit_solution(7150170784978559097)
XLA Ops:
  0.6 36.4 %section.1 = (f32[5,64,128]{2,1,0:T(8,128)S(1)}, f32[5,64,128]{2,1,0:T(8,128)S(1)}, f32[40,128]{1,0:T(8,128)S(1)}) custom-call(f32[64,128]{1,0:T(8,128)} %bitcast.12, f32[3,64,128]{2,1,0:T(8,128)} %bitcast.10, f32[64,128]{1,0:T(8,128)} %bitcast.13, bf16[5,64,128]{2,1,0:T(8,128)(2,1)} %bitcast.11, bf16[30,64]{1,0:T(8,128)(2,1)} %bitcast.14, ...), custom_call_target="tpu_custom_call" | custom-call | tf_op jit(solution)/shard_map/section/pallas_call | solution.py:559
  37.0 0.8 %store.1 = (f32[5,64,128]{2,1,0:T(8,128)}, f32[5,64,128]{2,1,0:T(8,128)}, f32[30,64]{1,0:T(8,128)}, f32[1,64]{1,0:T(1,128)}, f32[5,64]{1,0:T(8,128)}) custom-call(f32[5,64,128]{2,1,0:T(8,128)S(1)} %get-tuple-element.13.res, f32[5,64,128]{2,1,0:T(8,128)S(1)} %get-tuple-element.14.adj, f32[40,128]{1,0:T(8,128)S(1)} %get-tuple-element.15.grad), custom_call_target="tpu_custom_call" | custom-call | tf_op jit(solution)/shard_map/store/pallas_call | solution.py:595
